TPU v7x, 256 devices: a whole 4x4x8 slice. The times are simulated.
256 devices in a mesh: in: 8 (over x, z_lo), out: 32 (over y, z_hi, core).
Axes of the slice: x: 4, y: 4, z: 8 (z_hi: 4, z_lo: 2; z = z_hi * 2 + z_lo), core: 2. Of those that a mesh axis runs over, the one named last changes fastest.
Arguments:
- activations: bfloat16 [4096, 8192], P('out', 'in'), may hold values from -6 to 6
- cotangent: bfloat16 [4096, 28672], P('in', 'out'), may hold values from -0.09375 to 0.09375
- basis_in: float32 [8192, 512], P('in'), may hold values from -1 to 1, as said below
- basis_out: float32 [28672, 1024], P('out'), may hold values from -1 to 1, as said below
Outputs:
- projected: float32 [8192, 28672], P('in', 'out')
Inputs may be any that keep to these rules, and one draw needn't show every extreme that they name: The columns of basis_in are orthonormal. The columns of basis_out are orthonormal.
All inputs are finite; a program needn't handle non-finite values.
Results may differ from a plain program's by a relative error of at most 0.0003.
Values may be sent and summed in bfloat16 or wider, within the bound.
No kernel may reach another device: no remote copies, remote signals or barrier semaphores. Data moves between devices by JAX's collectives and lax.ppermute only.
A program may use at most 128 MiB of HBM per device.

v0:
```python
import jax
import jax.numpy as jnp
from jax import lax
from jax.sharding import PartitionSpec as P


def transposed_product(left, right):
    return lax.dot_general(
        left, right, (((0,), (0,)), ((), ())), preferred_element_type=jnp.float32
    )


def exact_product(left, right):
    return jnp.dot(left, right, precision=lax.Precision.HIGHEST, preferred_element_type=jnp.float32)


def exact_left_transposed(left, right):
    return lax.dot_general(
        left,
        right,
        (((0,), (0,)), ((), ())),
        precision=lax.Precision.HIGHEST,
        preferred_element_type=jnp.float32,
    )


def exact_right_transposed(left, right):
    return lax.dot_general(
        left,
        right,
        (((1,), (1,)), ((), ())),
        precision=lax.Precision.HIGHEST,
        preferred_element_type=jnp.float32,
    )


def per_device(activations, cotangent, basis_in, basis_out):
    cotangent_whole = lax.all_gather(cotangent, "in", axis=0, tiled=True)
    gradient = transposed_product(
        lax.all_gather(activations, "out", axis=0, tiled=True), cotangent_whole
    )
    row_coeff = lax.psum(exact_left_transposed(basis_in, gradient), "in")
    left_done = gradient - exact_product(basis_in, row_coeff)
    col_coeff = lax.psum(exact_product(left_done, basis_out), "out")
    projected = left_done - exact_right_transposed(col_coeff, basis_out)
    return projected


def solution(mesh):
    placed = (P("out", "in"), P("in", "out"), P("in", None), P("out", None))
    return jax.shard_map(
        per_device, mesh=mesh, in_specs=placed, out_specs=P("in", "out"), check_vma=False
    )
```

profile of v0, /device:TPU:1, one launch (start us, length us, event | category | flops | bytes accessed | tf_op | source)
XLA Modules:
  0.0 716.3 jit_solution(13889716682140816202)
XLA Ops:
  6.5 0.0 copy-start
  6.5 0.0 all-gather.5.cloned.1.call-start
  6.5 0.7 all-gather.5.cloned.1.call-update
  7.3 0.0 all-gather.3.cloned.1.call-start
  7.3 0.7 all-gather.3.cloned.1.call-update
  8.0 0.0 all-reduce.3.cloned.1.call-start
  8.1 156.2 %all-gather.5.cloned.1.call-done = bf16[4096,896]{1,0:T(8,128)(2,1)} async-done(((bf16[512,896]{1,0:T(8,128)(2,1)}), bf16[4096,896]{1,0:T(8,128)(2,1)}) %all-gather.5.cloned.1.call-update) | async-done | bytes 7340048 | tf_op jit(solution)/shard_map/all_gather | solution.py:38
  164.3 80.1 %all-gather.3.cloned.1.call-done = bf16[4096,1024]{1,0:T(8,128)(2,1)} async-done(((bf16[128,1024]{1,0:T(8,128)(2,1)}), bf16[4096,1024]{1,0:T(8,128)(2,1)}) %all-gather.3.cloned.1.call-update) | async-done | bytes 8388624 | tf_op jit(solution)/shard_map/all_gather | solution.py:40
  244.3 12.8 %fusion = f32[1024,896]{1,0:T(8,128)S(1)} fusion(bf16[4096,1024]{1,0:T(8,128)(2,1)} %all-gather.3.cloned.1.call-done, bf16[4096,896]{1,0:T(8,128)(2,1)} %all-gather.5.cloned.1.call-done), kind=kOutput, calls=%fused_computation.3 | convolution fusion | flops 7516192768 | bytes 19398656 | tf_op jit(solution)/shard_map/dot_general | solution.py:8
  257.2 0.0 copy-start.1
  257.2 1.8 copy-done.1
  259.0 0.0 copy-done
  259.0 7.2 %convolution_bitcast_fusion = f32[512,896]{0,1:T(8,128)} fusion(f32[1024,896]{1,0:T(8,128)S(1)} %fusion, f32[1024,512]{1,0:T(8,128)S(1)} %copy-done), kind=kOutput, calls=%fused_computation.2 | convolution fusion | flops 5637144576 | bytes 7602176 | tf_op jit(solution)/shard_map/dot_general | solution.py:18
  266.2 0.0 all-reduce.3.cloned.1.call-update
  266.2 0.2 all-reduce.5.cloned.1.call-start
  266.5 100.2 %all-reduce.3.cloned.1.call-done = f32[512,896]{0,1:T(8,128)} async-done(((f32[512,896]{0,1:T(8,128)}), f32[512,896]{0,1:T(8,128)}) %all-reduce.3.cloned.1.call-update) | async-done | bytes 1835024 | tf_op jit(solution)/shard_map/psum | solution.py:42
  366.6 0.0 copy-start.3
  366.6 10.3 %bitcast_subtract_fusion = f32[1024,896]{1,0:T(8,128)S(1)} fusion(f32[1024,896]{1,0:T(8,128)} %copy-done.1, f32[512,896]{0,1:T(8,128)} %all-reduce.3.cloned.1.call-done, f32[1024,512]{1,0:T(8,128)S(1)} %copy-done), kind=kOutput, calls=%fused_computation | convolution fusion | flops 5638062080 | bytes 11272192 | tf_op jit(solution)/shard_map/dot_general | solution.py:14
  377.0 0.0 copy-start.2
  377.0 1.8 copy-done.2
  378.8 0.0 copy-done.3
  378.8 14.7 %fusion.1 = f32[1024,1024]{1,0:T(8,128)} fusion(f32[1024,896]{1,0:T(8,128)S(1)} %bitcast_subtract_fusion, f32[896,1024]{1,0:T(8,128)S(1)} %copy-done.3), kind=kOutput, calls=%fused_computation.4 | convolution fusion | flops 11274289152 | bytes 11534336 | tf_op jit(solution)/shard_map/dot_general | solution.py:14
  393.5 0.0 all-reduce.5.cloned.1.call-update
  393.5 298.0 %all-reduce.5.cloned.1.call-done = f32[1024,1024]{1,0:T(8,128)} async-done(((f32[1024,1024]{1,0:T(8,128)}), f32[1024,1024]{1,0:T(8,128)}) %all-reduce.5.cloned.1.call-update) | async-done | bytes 4194320 | tf_op jit(solution)/shard_map/psum | solution.py:44
  691.5 18.2 %convolution_subtract_fusion = f32[1024,896]{1,0:T(8,128)} fusion(f32[1024,896]{1,0:T(8,128)} %copy-done.2, f32[1024,1024]{1,0:T(8,128)} %all-reduce.5.cloned.1.call-done, f32[896,1024]{1,0:T(8,128)} %param.7), kind=kOutput, calls=%fused_computation.1 | convolution fusion | flops 11275206656 | bytes 15204352 | tf_op jit(solution)/shard_map/dot_general | solution.py:28
Async XLA Ops:
  6.5 252.5 %copy-start = (f32[1024,512]{1,0:T(8,128)S(1)}, f32[1024,512]{1,0:T(8,128)}, u32[]{:S(2)}) copy-start(f32[1024,512]{1,0:T(8,128)} %param.6) | copy-start | bytes 6291460
  6.5 157.7 %all-gather.5.cloned.1.call-start = ((), (), s32[]{:S(2)}) async-start(), calls=%async_computation.1 | async-start | bytes 8257536 | tf_op jit(solution)/shard_map/all_gather | solution.py:38
  7.3 237.1 %all-gather.3.cloned.1.call-start = ((), (), s32[]{:S(2)}) async-start(), calls=%async_computation | async-start | bytes 8650752 | tf_op jit(solution)/shard_map/all_gather | solution.py:40
  8.0 358.6 %all-reduce.3.cloned.1.call-start = ((), (), s32[]{:S(2)}) async-start(), calls=%async_computation.2 | async-start | bytes 3670016 | tf_op jit(solution)/shard_map/psum | solution.py:42
  257.2 1.8 copy-start.1
  266.2 425.2 %all-reduce.5.cloned.1.call-start = ((), (), s32[]{:S(2)}) async-start(), calls=%async_computation.3 | async-start | bytes 8388608 | tf_op jit(solution)/shard_map/psum | solution.py:44
  366.6 12.2 %copy-start.3 = (f32[896,1024]{1,0:T(8,128)S(1)}, f32[896,1024]{1,0:T(8,128)}, u32[]{:S(2)}) copy-start(f32[896,1024]{1,0:T(8,128)} %param.7) | copy-start | bytes 11010052
  377.0 1.8 copy-start.2
Sparse Core Ops, SparseCore 0:
  9.1 155.0 all-gather.4
  166.8 77.4 all-gather.2
  266.4 100.2 all-reduce.2
  393.6 297.8 all-reduce.4
where the time goes:
time: 717 us; the launch traced here: 716 us
  waiting for transfers between devices  636 us (89%)
  matrix products  63.3 us (9%)
  between operations  13.2 us (2%)
    psum x1, waiting for transfers between devices, per_device(): col_coeff = lax.psum(exact_product(left_done, basis_out), 'out')  298 us
    all_gather x1, waiting for transfers between devices, per_device(): cotangent_whole = lax.all_gather(cotangent, 'in', axis=0, tiled=True)  156 us
    psum x1, waiting for transfers between devices, per_device(): row_coeff = lax.psum(exact_left_transposed(basis_in, gradient), 'in')  100 us
    all_gather x1, waiting for transfers between devices, per_device(): lax.all_gather(activations, 'out', axis=0, tiled=True)  80.1 us
    dot_general x2, matrix products, exact_product(): jnp.dot(left, right, precision=lax.Precision.HIGHEST, preferred_element_t...  25 us
    dot_general x1, matrix products, exact_right_transposed(): lax.dot_general(left, right, (((1,), (1,)), ((), ())), precision=lax.Prec...  18.2 us
  transfers between devices with their start and end apart: 4, of which 4 were waited for; matrix products, arithmetic and copies ran while one was open for 0% of the time, Pallas kernels for 0%

commit v1 on v0

v1 whole, which is shorter than its diff:
```python
import functools

import jax
import jax.numpy as jnp
from jax import lax
from jax.experimental import pallas as pl
from jax.experimental.pallas import tpu as pltpu
from jax.sharding import Mesh, PartitionSpec as P

SIZES = {"x": 4, "l": 2, "y": 4, "h": 4, "c": 2}
IN = ("x", "l")
OUT = ("y", "h", "c")
CHIPS = ("y", "h")
BF16, F32 = jnp.bfloat16, jnp.float32
ANY = pl.BlockSpec(memory_space=pltpu.HBM)
VMEM = pl.BlockSpec(memory_space=pltpu.VMEM)
SMEM = pl.BlockSpec(memory_space=pltpu.SMEM)
X, L, Y, H, C = range(5)


def shift(value, axis, step):
    size = SIZES[axis]
    return lax.ppermute(value, axis, [(k, (k + step) % size) for k in range(size)])


def spread(value, axes, count):
    return lax.all_to_all(jnp.broadcast_to(value, (count,) + value.shape), axes, 0, 0)


def dot(left, right, dims=((1,), (0,))):
    return lax.dot_general(left, right, (dims, ((), ())), preferred_element_type=F32)


def split(value):
    high = value.astype(BF16)
    return high, (value - high.astype(F32)).astype(BF16)


def three(left, right, dims=((1,), (0,))):
    lh, ll = split(left)
    rh, rl = split(right)
    return dot(lh, rh, dims) + (dot(lh, rl, dims) + dot(ll, rh, dims))


def encode(value):
    square = value * value
    return (square * value * jnp.abs(value)).astype(BF16)


def decode(code):
    wide = code.astype(F32)
    root = jnp.sqrt(jnp.sqrt(jnp.abs(wide)))
    return jnp.where(wide < 0, -root, root)


def call(kernel, out_shape, in_specs, scratch=(), flops=0, moved=0, **extra):
    return pl.pallas_call(
        kernel,
        out_shape=out_shape,
        in_specs=in_specs,
        out_specs=jax.tree.map(lambda _: VMEM, out_shape),
        scratch_shapes=list(scratch),
        compiler_params=pltpu.CompilerParams(vmem_limit_bytes=50 << 20),
        cost_estimate=pl.CostEstimate(flops=flops, bytes_accessed=moved, transcendentals=0),
        **extra,
    )


def shape(*dims, kind=F32):
    return jax.ShapeDtypeStruct(dims, kind)


def front_kernel(at, a_ref, c_ref, u_ref, v_ref, p_ref, mine_ref, theirs_ref):
    c = c_ref[...]
    for out_ref, which in ((theirs_ref, 1 - at[C]), (mine_ref, at[C])):
        high, low = split(v_ref[:, pl.ds(pl.multiple_of(which * 512, 512), 512)])
        out_ref[...] = (dot(c, high) + dot(c, low)).T
    high, low = split(u_ref[...])
    a = a_ref[...]
    p_ref[...] = (dot(a, high) + dot(a, low)).T


def front(at, a, c, u, v):
    return call(
        front_kernel,
        (shape(512, 128), shape(512, 512), shape(512, 512)),
        [SMEM] + [VMEM] * 4,
        flops=4 * 512 * 896 * 1024 + 4 * 128 * 1024 * 512,
        moved=10 << 20,
    )(at, a, c, u, v)


def prepare_kernel(at, v_ref, high_ref, low_ref):
    for n, which in enumerate((at[C], 1 - at[C])):
        turned = v_ref[:, pl.ds(pl.multiple_of(which * 512, 512), 512)].T
        high, low = split(turned)
        high_ref[512 * n : 512 * n + 512, :] = high
        low_ref[512 * n : 512 * n + 512, :] = low


def prepare(at, v):
    return call(
        prepare_kernel, (shape(1024, 896, kind=BF16), shape(1024, 896, kind=BF16)), [SMEM, VMEM], moved=8 << 20
    )(at, v)


def run(copies, sems):
    started = [pltpu.make_async_copy(src, dst, sems.at[k]) for k, (src, dst) in enumerate(copies)]
    for copy in started:
        copy.start()
    for copy in started:
        copy.wait()


def sems(count):
    return pltpu.SemaphoreType.DMA((count,))


def second_kernel(left, right, mate, a, p, *rest):
    xp, xm, a_out, p_out, sem = rest[-5:]
    run(
        [
            (left.at[pl.ds(0, 256)], xp.at[pl.ds(0, 256)]),
            (mate, xp.at[pl.ds(256, 512)]),
            (right.at[pl.ds(256, 256)], xm.at[pl.ds(0, 256)]),
            (mate, xm.at[pl.ds(256, 512)]),
            (a, a_out),
            (p, p_out),
        ],
        sem,
    )


def third_kernel(xp, xm, a, hp, hm, h2, *rest):
    far, column, sem = rest[-3:]
    copies = [(xp.at[pl.ds(0, 256)], far.at[pl.ds(0, 256)]), (xm.at[pl.ds(0, 256)], far.at[pl.ds(256, 256)])]
    run(copies + [(ref, column.at[k]) for k, ref in enumerate((a, hp, hm, h2))], sem)


def assemble(kernel, outs, count, operands, after):
    return pl.pallas_call(
        kernel,
        out_shape=outs,
        in_specs=[ANY] * (len(operands) + len(after)),
        out_specs=tuple(VMEM for _ in outs),
        scratch_shapes=[sems(count)],
        compiler_params=pltpu.CompilerParams(vmem_limit_bytes=50 << 20),
        cost_estimate=pl.CostEstimate(flops=0, bytes_accessed=8 << 20, transcendentals=0),
    )(*operands, *after)


def coefficients_kernel(at, q_ref, own_ref, other_ref, here_ref, there_ref, p2_ref, t_ref):
    core = at[C]
    q = jnp.concatenate([q_ref[k] for k in range(8)], axis=1)
    for b in range(16):
        one, two = q[:, 256 * b : 256 * b + 128], q[:, 256 * b + 128 : 256 * b + 256]
        where = slice(128 * b, 128 * b + 128)
        here_ref[:, where] = jnp.where(core == 0, one, two)
        there_ref[:, where] = jnp.where(core == 0, two, one)
    for n, ref in enumerate((own_ref, other_ref)):
        for k in range(16):
            high, low = split(ref[k])
            where = slice(2048 * n + 128 * k, 2048 * n + 128 * k + 128)
            p2_ref[:64, where] = high
            p2_ref[64:, where] = low
    nt = ((1,), (1,))
    t = 0.0
    for n, ref in enumerate((here_ref, there_ref)):
        where = slice(2048 * n, 2048 * n + 2048)
        qh, ql = split(ref[...])
        ph, pl_ = p2_ref[:64, where], p2_ref[64:, where]
        t = t + (dot(qh, ph, nt) + (dot(qh, pl_, nt) + dot(ql, ph, nt)))
    t_ref[...] = t


def coefficients(at, q, own, other):
    return call(
        coefficients_kernel,
        (shape(32, 2048), shape(32, 2048), shape(128, 4096, kind=BF16), shape(32, 64)),
        [SMEM] + [VMEM] * 3,
        flops=6 * 32 * 64 * 4096,
        moved=4 << 20,
    )(at, q, own, other)


CPIECES = (
    ((0, 512, 0, 0, 0),),
    ((0, 512, 0, 1, 0),),
    ((0, 512, 3, 0, 0),),
    ((0, 512, 1, 0, 0),),
    ((0, 256, 2, 0, 0), (256, 512, 3, 1, 0)),
    ((0, 256, 2, 0, 256), (256, 512, 1, 1, 0)),
    ((0, 512, 2, 1, 0),),
)


def activation_copies(at, refs, whole):
    copies = []
    for ref, dy in zip(refs, (0, 3, 1, 2)):
        for k, dh in enumerate((0, 3, 1, 2)):
            block = lax.rem(at[Y] + dy, 4) * 4 + lax.rem(at[H] + dh, 4)
            copies.append((ref.at[k], whole.at[:, pl.ds(pl.multiple_of(block * 128, 128), 128)]))
    return copies


def half_copies(at, refs, whole, core):
    copies = []
    for ref, parts in zip(refs, CPIECES):
        for row, rows, dx, dl, first in parts:
            shard = lax.rem(at[X] + dx, 4) * 2 + lax.rem(at[L] + dl, 2)
            for n in range(rows // 256):
                src = ref.at[pl.ds(pl.multiple_of(row + 256 * n + 128 * core, 128), 128)]
                dst = whole.at[pl.ds(pl.multiple_of(shard * 256 + first // 2 + 128 * n, 128), 128)]
                copies.append((src, dst))
    return copies


def s_kernel(at, here_ref, there_ref, *rest):
    refs = rest[:4]
    own_ref, other_ref, whole, sem = rest[-4:]
    run(activation_copies(at, refs, whole), sem)
    rows = jnp.concatenate(split(here_ref[...]) + split(there_ref[...]), axis=0)
    s = dot(rows, whole[...], ((1,), (1,)))
    own_ref[...] = s[:32] + s[32:64]
    other_ref[...] = s[64:96] + s[96:]


def s_parts(at, here, there, pieces, after):
    return call(
        s_kernel, (shape(32, 1024), shape(32, 1024), shape(1024, 2048, kind=BF16)),
        [SMEM] + [VMEM] * 2 + [ANY] * (4 + len(after)), (sems(16),),
        flops=2 * 128 * 2048 * 1024, moved=10 << 20,
    )(at, here, there, *pieces, *after)


def cross_kernel(t_ref, u_ref, out_ref):
    t = jnp.concatenate([t_ref[k] for k in range(8)], axis=1)
    out_ref[...] = three(t, u_ref[...], ((1,), (1,)))


def cross(t, u):
    return call(cross_kernel, shape(32, 1024), [VMEM] * 2, flops=6 * 32 * 512 * 1024, moved=3 << 20)(t, u)


def code_kernel(own_ref, other_ref, cross_ref, out_ref):
    out_ref[...] = encode(own_ref[...] + other_ref[...] - cross_ref[...])


def s_code(own, other, taken):
    return call(code_kernel, shape(32, 1024, kind=BF16), [VMEM] * 3, moved=1 << 20)(own, other, taken)


def touch_kernel(*refs):
    pass


def touch(value, after):
    return pl.pallas_call(
        touch_kernel, out_shape=shape(*value.shape, kind=value.dtype), in_specs=[ANY] * 2, out_specs=ANY,
        input_output_aliases={0: 0},
    )(value, after)


def turn_kernel(at, *rest):
    pieces, out_ref, whole = rest[:4], rest[-2], rest[-1]
    for ref, dy in zip(pieces, (0, 3, 1, 2)):
        for k, dh in enumerate((0, 3, 1, 2)):
            block = lax.rem(at[Y] + dy, 4) * 4 + lax.rem(at[H] + dh, 4)
            whole[pl.ds(pl.multiple_of(block * 32, 32), 32), :] = ref[k]
    for k in range(8):
        out_ref[128 * k : 128 * k + 128, :] = whole[:, 128 * k : 128 * k + 128].T


def turn(at, pieces, after):
    return call(
        turn_kernel, shape(1024, 512, kind=BF16), [SMEM] + [VMEM] * 4 + [ANY] * len(after),
        (pltpu.VMEM((512, 1024), BF16),), moved=3 << 20,
    )(at, *pieces, *after)


def r_kernel(at, p_ref, *rest):
    refs, (out_ref, own_ref, other_ref, sem) = rest[:7], rest[-4:]
    copies = half_copies(at, refs, own_ref, at[C]) + half_copies(at, refs, other_ref, 1 - at[C])
    run(copies, sem)
    r = dot(p_ref[:, :2048], own_ref[...]) + dot(p_ref[:, 2048:], other_ref[...])
    code = encode(r[:64] + r[64:])
    for n in range(8):
        out_ref[n] = code


def r_slices(at, p2, pieces):
    half = shape(2048, 896, kind=BF16)
    return call(
        r_kernel, (shape(8, 64, 896, kind=BF16), half, half), [SMEM, VMEM] + [ANY] * 7, (sems(32),),
        flops=2 * 128 * 4096 * 896, moved=12 << 20,
    )(at, p2, *pieces)


def final_kernel(g_ref, u_ref, r_ref, own_ref, other_ref, high_ref, low_ref, out_ref, rh_ref, rl_ref):
    @pl.when(pl.program_id(0) == 0)
    def _():
        high, low = split(decode(r_ref[...]))
        rh_ref[:512, :] = high
        rl_ref[:512, :] = low
        rh_ref[512:, :] = high_ref[...]
        rl_ref[512:, :] = low_ref[...]

    parts = [u_ref[...], decode(own_ref[...]), decode(other_ref[...])]
    highs, lows = zip(*map(split, parts))
    high, low = jnp.concatenate(highs, axis=1), jnp.concatenate(lows, axis=1)
    out_ref[...] = g_ref[...] - (dot(high, rh_ref[...]) + (dot(high, rl_ref[...]) + dot(low, rh_ref[...])))


def final(g, u, r, own, other, high, low):
    def rows(width):
        return pl.BlockSpec((512, width), lambda k: (k, 0))

    def whole(height):
        return pl.BlockSpec((height, 896), lambda k: (0, 0), pipeline_mode=pl.Buffered(1))

    return pl.pallas_call(
        final_kernel,
        grid=(2,),
        in_specs=[rows(896), rows(512), whole(512), rows(512), rows(512), whole(1024), whole(1024)],
        out_specs=rows(896),
        out_shape=shape(1024, 896),
        scratch_shapes=[pltpu.VMEM((1536, 896), BF16)] * 2,
        compiler_params=pltpu.CompilerParams(vmem_limit_bytes=50 << 20),
        cost_estimate=pl.CostEstimate(flops=6 * 1024 * 896 * 1536, bytes_accessed=16 << 20, transcendentals=0),
    )(g, u, r, own, other, high, low)


def add_up(parts):
    return jnp.sum(parts, axis=0)


def per_device(a, c, u, v):
    at = jnp.stack([lax.axis_index(n) for n in SIZES]).astype(jnp.int32)
    a_turned = a.T
    left, right, mate = shift(c, "x", 1), shift(c, "x", -1), shift(c, "l", 1)
    p, mine, theirs = front(at, a, c, u, v)
    q = mine + shift(theirs, "c", 1)
    q = add_up(lax.all_to_all(q.reshape(4, 128, 512), "y", 0, 0))

    strip = shape(768, 896, kind=BF16)
    xp, xm, a_turned, p = assemble(
        second_kernel, (strip, strip, shape(1024, 128, kind=BF16), shape(512, 128)), 6,
        (left, right, mate, a_turned, p), (q,),
    )
    xp, xm = shift(xp, "x", 1), shift(xm, "x", -1)
    hp, hm, h2 = shift(a_turned, "h", 1), shift(a_turned, "h", -1), shift(a_turned, "h", 2)
    p = add_up(lax.all_to_all(p.reshape(8, 64, 128), IN, 0, 0))
    q = add_up(lax.all_to_all(q.reshape(4, 32, 512), "h", 0, 0))

    far, column = assemble(
        third_kernel, (shape(512, 896, kind=BF16), shape(4, 1024, 128, kind=BF16)), 6,
        (xp, xm, a_turned, hp, hm, h2), (q, p),
    )
    far = shift(far, "l", 1)
    apieces = [column] + [shift(column, "y", step) for step in (1, -1, 2)]
    q = spread(q, IN, 8)
    p_own = spread(p, CHIPS, 16)
    here, there, p2, t = coefficients(at, q, p_own, shift(p_own, "c", 1))
    there = shift(there, "c", 1)
    taken = cross(spread(t, IN, 8), u)
    vh, vl = prepare(at, v)
    r, c_own, c_other = r_slices(at, p2, (c, mate, left, right, xp, xm, far))
    r = lax.all_to_all(r, IN, 0, 0).reshape(512, 896)

    s, s_other, a_own = s_parts(at, here, there, apieces, (taken, vh, c_own))
    s = s_code(s, shift(s_other, "c", 1), taken)
    a_own = touch(a_own, s)
    column = jnp.stack([s, shift(s, "h", 1), shift(s, "h", -1), shift(s, "h", 2)])
    spieces = [column] + [shift(column, "y", step) for step in (1, -1, 2)]
    g = dot(a_own, c_own) + dot(shift(a_own, "c", 1), c_other)
    s = turn(at, spieces, (g, r))
    return final(g, u, r, s, shift(s, "c", 1), vh, vl)


def solution(mesh):
    fine = Mesh(mesh.devices.reshape(tuple(SIZES.values())), tuple(SIZES))
    placed = (P(OUT, IN), P(IN, OUT), P(IN, None), P(OUT, None))
    return jax.shard_map(per_device, mesh=fine, in_specs=placed, out_specs=P(IN, OUT), check_vma=False)
```

time: 717 us -> 220 us (0.31)
  waiting for transfers between devices: 636 us -> 58.8 us
  starting transfers between devices: 0.3 us -> 69 us
  Pallas kernels: 0 us -> 49.6 us
  matrix products: 63.3 us -> 13.8 us
  between operations: 13.2 us -> 0.31 us
  blocking collectives: 0 us -> 9.76 us
  local copies, waits for them, and re-layouts: 3.67 us -> 11.5 us
    psum x2 -> x0, waiting for transfers between devices: 398 us -> none  [the longest x1 298 us: per_device(): col_coeff = lax.psum(exact_product(left_done, basis_out), 'out')]
    all_gather x2 -> x0, waiting for transfers between devices: 236 us -> none  [the longest x1 156 us: per_device(): cotangent_whole = lax.all_gather(cotangent, 'in', axis=0, tiled=True)]
    pallas_call x0 -> x12, Pallas kernels: none -> 49.6 us  [the longest x1 17.8 us: final(): pl.pallas_call(final_kernel, grid=(2,), in_specs=[rows(896), rows(512), w...]
    dot_general x5 -> x2, matrix products: 63.3 us -> 13.8 us  [dot(): lax.dot_general(left, right, (dims, ((), ())), preferred_element_type=F32)]
    all_to_all x0 -> x6, waiting for transfers between devices: none -> 42.9 us  [the longest x3 24.6 us: spread(): lax.all_to_all(jnp.broadcast_to(value, (count,) + value.shape), axes, 0, 0)]
    ppermute x0 -> x24, starting transfers between devices: none -> 39.6 us  [shift(): lax.ppermute(value, axis, [(k, (k + step) % size) for k in range(size)])]
    all_to_all x0 -> x6, starting transfers between devices: none -> 29.4 us  [the longest x3 14.6 us: spread(): lax.all_to_all(jnp.broadcast_to(value, (count,) + value.shape), axes, 0, 0)]
    ppermute x0 -> x24, waiting for transfers between devices: none -> 15.9 us  [shift(): lax.ppermute(value, axis, [(k, (k + step) % size) for k in range(size)])]
  transfers between devices with their start and end apart: 4 -> 30, of which waited for: 4 -> 10; matrix products, arithmetic and copies ran while one was open for 0% -> 11% of each run, Pallas kernels for 0% -> 8%
where the time goes in v1:
time: 220 us; the launch traced here: 219 us
  starting transfers between devices  69 us (31%)
  waiting for transfers between devices  58.8 us (27%)
  Pallas kernels  49.6 us (23%)
  matrix products  13.8 us (6%)
  local copies, waits for them, and re-layouts  11.5 us (5%)
  blocking collectives  9.76 us (4%)
  other arithmetic  6.02 us (3%)
    ppermute x24, starting transfers between devices, shift(): lax.ppermute(value, axis, [(k, (k + step) % size) for k in range(size)])  39.6 us
    all_to_all x3, waiting for transfers between devices, spread(): lax.all_to_all(jnp.broadcast_to(value, (count,) + value.shape), axes, 0, 0)  24.6 us
    pallas_call x1, Pallas kernels, final(): pl.pallas_call(final_kernel, grid=(2,), in_specs=[rows(896), rows(512), w...  17.8 us
    ppermute x24, waiting for transfers between devices, shift(): lax.ppermute(value, axis, [(k, (k + step) % size) for k in range(size)])  15.9 us
    all_to_all x3, starting transfers between devices, spread(): lax.all_to_all(jnp.broadcast_to(value, (count,) + value.shape), axes, 0, 0)  14.6 us
    all_to_all x1, waiting for transfers between devices, per_device(): q = add_up(lax.all_to_all(q.reshape(4, 128, 512), 'y', 0, 0))  13.9 us
    dot_general x2, matrix products, dot(): lax.dot_general(left, right, (dims, ((), ())), preferred_element_type=F32)  13.8 us
    all_to_all x1, blocking collectives, per_device(): p = add_up(lax.all_to_all(p.reshape(8, 64, 128), IN, 0, 0))  9.76 us
  transfers between devices with their start and end apart: 30, of which 10 were waited for; matrix products, arithmetic and copies ran while one was open for 11% of the time, Pallas kernels for 8%

profile of v1, /device:TPU:1, one launch (start us, length us, event | category | flops | bytes accessed | tf_op | source)
XLA Modules:
  0.0 218.9 jit_solution(16537370867182050630)
XLA Ops:
  0.1 0.9 copy-done.6
  1.0 5.8 %shard_map.46 = (f32[512,128]{1,0:T(8,128)S(1)}, f32[512,512]{1,0:T(8,128)S(1)}, f32[512,512]{1,0:T(8,128)S(1)}) custom-call(s32[5]{0:T(128)S(1)} %stack.38.at, bf16[128,1024]{1,0:T(8,128)(2,1)S(1)} %copy-done.6, bf16[512,896]{1,0:T(8,128)(2,1)} %rest_0_.1, f32[1024,512]{1,0:T(8,128)} %u_ref.5, f32[896,1024]{1,0:T(8,128)} %v_ref.3), custom_call_target="tpu_custom_call" | custom-call | flops 2147483648 | bytes 10485760 | tf_op jit(solution)/shard_map/pallas_call | solution.py:84
  6.8 3.3 %collective-permute-start = (f32[512,512]{1,0:T(8,128)S(1)}, f32[512,512]{1,0:T(8,128)S(1)}, u32[]{:S(2)}, u32[]{:S(2)}) collective-permute-start(f32[512,512]{1,0:T(8,128)S(1)} %get-tuple-element.27), channel_id=1, source_target_pairs={{0,1},{1,0},{2,3},{3,2},{4,5},{5,4},{6,7},{7,6},{8,9},{9,8},{10,11... | collective-permute-start | bytes 3145736 | tf_op jit(solution)/shard_map/ppermute | solution.py:23
  10.1 2.7 %collective-permute-start.2 = (bf16[512,896]{1,0:T(8,128)(2,1)}, bf16[512,896]{1,0:T(8,128)(2,1)S(1)}, u32[]{:S(2)}, u32[]{:S(2)}) collective-permute-start(bf16[512,896]{1,0:T(8,128)(2,1)} %rest_0_.1), channel_id=1, source_target_pairs={{0,192},{64,0},{128,64},{192,128},{1,193},{65,1},{129,65},{193,129... | collective-permute-start | bytes 2752520 | tf_op jit(solution)/shard_map/ppermute | solution.py:23
  12.8 1.2 add.6
  14.0 4.2 %all-to-all-start = ((f32[4,128,512]{2,1,0:T(8,128)}), f32[4,128,512]{2,1,0:T(8,128)}, u32[]{:S(2)}, u32[]{:S(2)}) async-start(f32[4,128,512]{2,1,0:T(8,128)} %bitcast.23), calls=%async_computation | async-start | bytes 2097152 | tf_op jit(solution)/shard_map/all_to_all | solution.py:343
  18.5 13.9 %all-to-all-done = f32[4,128,512]{2,1,0:T(8,128)} async-done(((f32[4,128,512]{2,1,0:T(8,128)}), f32[4,128,512]{2,1,0:T(8,128)}, u32[]{:S(2)}, u32[]{:S(2)}) %all-to-all-start) | async-done | bytes 1048608 | tf_op jit(solution)/shard_map/all_to_all | solution.py:343
  32.4 2.0 reduce_sum.27.rest_0_
  34.4 2.6 %shard_map.47 = (bf16[768,896]{1,0:T(8,128)(2,1)}, bf16[768,896]{1,0:T(8,128)(2,1)}, bf16[1024,128]{1,0:T(8,128)(2,1)S(1)}, f32[512,128]{1,0:T(8,128)S(1)}) custom-call(bf16[512,896]{1,0:T(8,128)(2,1)S(1)} %collective-permute-done.1.left.rest_2_, bf16[512,896]{1,0:T(8,128)(2,1)S(1)} %collective-permute-done.2.right.rest_3_, ...), custom_call_target="tpu_custom_call" | custom-call | bytes 8388608 | tf_op jit(solution)/shard_map/pallas_call | solution.py:141
  37.1 9.8 %all_to_all.35 = f32[8,64,128]{2,1,0:T(8,128)} all-to-all(f32[8,64,128]{2,1,0:T(8,128)S(1)} %bitcast.22), channel_id=1, replica_groups=mesh['x'=4,'l'=2,'y'=4,'h'=4,'c'=2] {'x','l'}, dimensions={0} | all-to-all | bytes 524288 | tf_op jit(solution)/shard_map/all_to_all | solution.py:352
  46.9 6.8 %all-to-all-start.1 = ((f32[4,32,512]{2,1,0:T(8,128)}), f32[4,32,512]{2,1,0:T(8,128)S(1)}, u32[]{:S(2)}, u32[]{:S(2)}) async-start(f32[4,32,512]{2,1,0:T(8,128)} %bitcast.6), calls=%async_computation.1 | async-start | bytes 524288 | tf_op jit(solution)/shard_map/all_to_all | solution.py:353
  53.6 2.7 %collective-permute-start.7 = (bf16[768,896]{1,0:T(8,128)(2,1)}, bf16[768,896]{1,0:T(8,128)(2,1)}, u32[]{:S(2)}, u32[]{:S(2)}) collective-permute-start(bf16[768,896]{1,0:T(8,128)(2,1)} %get-tuple-element.33), channel_id=1, source_target_pairs={{0,192},{64,0},{128,64},{192,128},{1,193},{65,1},{129,65},{193,129... | collective-permute-start | bytes 4128776 | tf_op jit(solution)/shard_map/ppermute | solution.py:23
  56.3 1.0 reduce_sum.29.rest_1_
  57.3 4.4 %all-to-all-done.1 = f32[4,32,512]{2,1,0:T(8,128)S(1)} async-done(((f32[4,32,512]{2,1,0:T(8,128)}), f32[4,32,512]{2,1,0:T(8,128)S(1)}, u32[]{:S(2)}, u32[]{:S(2)}) %all-to-all-start.1) | async-done | bytes 262176 | tf_op jit(solution)/shard_map/all_to_all | solution.py:353
  61.6 0.9 broadcast_in_dim.10
  62.6 4.8 %all-to-all-start.4 = ((f32[16,64,128]{2,1,0:T(8,128)}), f32[16,64,128]{2,1,0:T(8,128)S(1)}, u32[]{:S(2)}, u32[]{:S(2)}) async-start(f32[16,64,128]{2,1,0:T(8,128)} %broadcast_in_dim.10), calls=%async_computation.4 | async-start | bytes 1048576 | tf_op jit(solution)/shard_map/all_to_all | solution.py:27
  67.4 2.3 %collective-permute-start.8 = (bf16[1024,128]{1,0:T(8,128)(2,1)}, bf16[1024,128]{1,0:T(8,128)(2,1)}, u32[]{:S(2)}, u32[]{:S(2)}) collective-permute-start(bf16[1024,128]{1,0:T(8,128)(2,1)} %copy-done.8), channel_id=1, source_target_pairs={{0,2},{2,4},{4,6},{6,0},{1,3},{3,5},{5,7},{7,1},{8,10},{10,12},{12... | collective-permute-start | bytes 786440 | tf_op jit(solution)/shard_map/ppermute | solution.py:23
  69.6 1.4 collective-permute-start.9
  71.0 5.2 %collective-permute-start.10 = (bf16[1024,128]{1,0:T(8,128)(2,1)}, bf16[1024,128]{1,0:T(8,128)(2,1)}, u32[]{:S(2)}, u32[]{:S(2)}) collective-permute-start(bf16[1024,128]{1,0:T(8,128)(2,1)} %copy-done.8), channel_id=1, source_target_pairs={{0,4},{2,6},{4,0},{6,2},{1,5},{3,7},{5,1},{7,3},{8,12},{10,14},{12... | collective-permute-start | bytes 786440 | tf_op jit(solution)/shard_map/ppermute | solution.py:23
  76.2 1.0 reduce_sum.28.rest_0_
  77.2 20.8 %all-to-all-done.4.own_ref = f32[16,64,128]{2,1,0:T(8,128)S(1)} async-done(((f32[16,64,128]{2,1,0:T(8,128)}), f32[16,64,128]{2,1,0:T(8,128)S(1)}, u32[]{:S(2)}, u32[]{:S(2)}) %all-to-all-start.4) | async-done | bytes 524320 | tf_op jit(solution)/shard_map/all_to_all | solution.py:27
  98.0 0.9 broadcast_in_dim.9
  98.8 6.0 %all-to-all-start.2 = ((f32[8,32,512]{2,1,0:T(8,128)}), f32[8,32,512]{2,1,0:T(8,128)S(1)}, u32[]{:S(2)}, u32[]{:S(2)}) async-start(f32[8,32,512]{2,1,0:T(8,128)} %broadcast_in_dim.9), calls=%async_computation.2 | async-start | bytes 1048576 | tf_op jit(solution)/shard_map/all_to_all | solution.py:27
  104.8 0.9 copy-done.9
  105.8 2.7 %shard_map.49 = (bf16[512,896]{1,0:T(8,128)(2,1)}, bf16[4,1024,128]{2,1,0:T(8,128)(2,1)}) custom-call(bf16[768,896]{1,0:T(8,128)(2,1)} %collective-permute-done.6.xp.rest_4_, bf16[768,896]{1,0:T(8,128)(2,1)} %collective-permute-done.7.xm.rest_5_, bf16[1024,128]{1,0:T(8,128)(2,1)S(1)} %copy-done.9, bf16[1024,128]{1,0:T(8,128)(2,1)} %collective-permute-done.8.hp, ...), custom_call_target="tpu_custom_call" | custom-call | bytes 8388608 | tf_op jit(solution)/shard_map/pallas_call | solution.py:141
  108.5 1.0 collective-permute-start.11
  109.5 1.8 collective-permute-start.12
  111.3 1.2 collective-permute-start.13
  112.5 0.7 collective-permute-start.14
  113.2 2.5 %collective-permute-start.4 = (f32[16,64,128]{2,1,0:T(8,128)S(1)}, f32[16,64,128]{2,1,0:T(8,128)}, u32[]{:S(2)}, u32[]{:S(2)}) collective-permute-start(f32[16,64,128]{2,1,0:T(8,128)S(1)} %all-to-all-done.4.own_ref), channel_id=1, source_target_pairs={{0,1},{1,0},{2,3},{3,2},{4,5},{5,4},{6,7},{7,6},{8,9},{9,8},{10,11... | collective-permute-start | bytes 1572872 | tf_op jit(solution)/shard_map/ppermute | solution.py:23
  115.7 1.7 collective-permute-done.4.other_ref
  117.4 1.8 shard_map.48
  119.2 1.0 copy-done.3
  120.2 0.4 collective-permute-start.5
  120.6 0.7 reshape.16
  121.3 3.8 %all-to-all-start.5 = ((f32[8,1,2048]{2,1,0:T(1,128)}), f32[8,1,2048]{2,1,0:T(1,128)S(1)}, u32[]{:S(2)}, u32[]{:S(2)}) async-start(f32[8,1,2048]{2,1,0:T(1,128)} %reshape.16), calls=%async_computation.5 | async-start | bytes 131072 | tf_op jit(solution)/shard_map/all_to_all | solution.py:27
  125.1 3.1 %shard_map.51 = (bf16[1024,896]{1,0:T(8,128)(2,1)S(1)}, bf16[1024,896]{1,0:T(8,128)(2,1)S(1)}) custom-call(s32[5]{0:T(128)S(1)} %stack.38.at, f32[896,1024]{1,0:T(8,128)} %v_ref.3), custom_call_target="tpu_custom_call" | custom-call | bytes 8388608 | tf_op jit(solution)/shard_map/pallas_call | solution.py:102
  128.2 1.2 copy-done.2
  129.4 1.2 copy-done.10
  130.7 3.8 %all-to-all-done.5 = f32[8,1,2048]{2,1,0:T(1,128)S(1)} async-done(((f32[8,1,2048]{2,1,0:T(1,128)}), f32[8,1,2048]{2,1,0:T(1,128)S(1)}, u32[]{:S(2)}, u32[]{:S(2)}) %all-to-all-start.5) | async-done | bytes 65568 | tf_op jit(solution)/shard_map/all_to_all | solution.py:27
  134.5 0.6 broadcast
  135.1 0.8 reduce
  136.0 1.6 copy-done.1
  137.6 1.0 shard_map.50.rest_4_.cross_ref
  138.7 9.0 %shard_map.52 = (bf16[8,64,896]{2,1,0:T(8,128)(2,1)}, bf16[2048,896]{1,0:T(8,128)(2,1)}, bf16[2048,896]{1,0:T(8,128)(2,1)}) custom-call(s32[5]{0:T(128)S(1)} %stack.38.at, bf16[128,4096]{1,0:T(8,128)(2,1)} %copy-done.3, bf16[512,896]{1,0:T(8,128)(2,1)} %rest_0_.1, bf16[512,896]{1,0:T(8,128)(2,1)S(1)} %collective-permute-done.3.mate.rest_1_, ...), custom_call_target="tpu_custom_call" | custom-call | flops 939524096 | bytes 12582912 | tf_op jit(solution)/shard_map/pallas_call | solution.py:293
  147.7 8.9 %collective-permute-done.13.rest_3_ = bf16[4,1024,128]{2,1,0:T(8,128)(2,1)} collective-permute-done((bf16[4,1024,128]{2,1,0:T(8,128)(2,1)}, bf16[4,1024,128]{2,1,0:T(8,128)(2,1)}, u32[]{:S(2)}, u32[]{:S(2)}) %collective-permute-start.13) | collective-permute-done | bytes 1048608 | tf_op jit(solution)/shard_map/ppermute | solution.py:23
  156.7 4.8 %shard_map.53 = (f32[32,1024]{1,0:T(8,128)S(1)}, f32[32,1024]{1,0:T(8,128)S(1)}, bf16[1024,2048]{1,0:T(8,128)(2,1)}) custom-call(s32[5]{0:T(128)S(1)} %stack.38.at, f32[32,2048]{1,0:T(8,128)S(1)} %get-tuple-element.30.here_ref, f32[32,2048]{1,0:T(8,128)S(1)} %collective-permute-done.5.there_ref, bf16[4,1024,128]{2,1,0:T(8,128)(2,1)} %get-tuple-element.35.rest_0_, ...), custom_call_target="tpu_custom_call" | custom-call | flops 536870912 | bytes 10485760 | tf_op jit(solution)/shard_map/pallas_call | solution.py:229
  161.5 2.2 %collective-permute-start.15 = (f32[32,1024]{1,0:T(8,128)S(1)}, f32[32,1024]{1,0:T(8,128)S(1)}, u32[]{:S(2)}, u32[]{:S(2)}) collective-permute-start(f32[32,1024]{1,0:T(8,128)S(1)} %get-tuple-element.43), channel_id=1, source_target_pairs={{0,1},{1,0},{2,3},{3,2},{4,5},{5,4},{6,7},{7,6},{8,9},{9,8},{10,11... | collective-permute-start | bytes 393224 | tf_op jit(solution)/shard_map/ppermute | solution.py:23
  163.7 1.0 collective-permute-done.15.other_ref
  164.7 0.6 copy-done.4
  165.7 0.5 copy-done.5
  166.2 3.3 %collective-permute-start.19 = (bf16[32,1024]{1,0:T(8,128)(2,1)S(1)}, bf16[32,1024]{1,0:T(8,128)(2,1)S(1)}, u32[]{:S(2)}, u32[]{:S(2)}) collective-permute-start(bf16[32,1024]{1,0:T(8,128)(2,1)S(1)} %copy-done.5), channel_id=1, source_target_pairs={{0,4},{2,6},{4,0},{6,2},{1,5},{3,7},{5,1},{7,3},{8,12},{10,14},{12... | collective-permute-start | bytes 196616 | tf_op jit(solution)/shard_map/ppermute | solution.py:23
  169.5 3.3 %collective-permute-start.18 = (bf16[32,1024]{1,0:T(8,128)(2,1)S(1)}, bf16[32,1024]{1,0:T(8,128)(2,1)S(1)}, u32[]{:S(2)}, u32[]{:S(2)}) collective-permute-start(bf16[32,1024]{1,0:T(8,128)(2,1)S(1)} %copy-done.5), channel_id=1, source_target_pairs={{0,6},{2,0},{4,2},{6,4},{1,7},{3,1},{5,3},{7,5},{8,14},{10,8},{12,... | collective-permute-start | bytes 196616 | tf_op jit(solution)/shard_map/ppermute | solution.py:23
  172.8 3.8 %all-to-all-start.6 = ((bf16[8,64,896]{2,1,0:T(8,128)(2,1)}), bf16[8,64,896]{2,1,0:T(8,128)(2,1)S(1)}, u32[]{:S(2)}, u32[]{:S(2)}) async-start(bf16[8,64,896]{2,1,0:T(8,128)(2,1)} %get-tuple-element.45), calls=%async_computation.6 | async-start | bytes 1835008 | tf_op jit(solution)/shard_map/all_to_all | solution.py:368
  176.7 0.9 collective-permute-done.18
  177.5 1.1 collective-permute-done.17
  178.7 0.8 collective-permute-start.20
  179.5 2.0 collective-permute-start.21
  181.4 7.5 %fusion = f32[1024,896]{1,0:T(8,128)S(1)} fusion(bf16[1024,2048]{1,0:T(8,128)(2,1)} %collective-permute-done.16, bf16[2048,896]{1,0:T(8,128)(2,1)} %get-tuple-element.44), kind=kOutput, calls=%fused_computation.2 | convolution fusion | flops 3758096384 | bytes 11534336 | tf_op jit(solution)/shard_map/dot_general | solution.py:31
  189.0 6.3 %convolution_add_fusion.rest_4_.g_ref = f32[1024,896]{1,0:T(8,128)} fusion(f32[1024,896]{1,0:T(8,128)S(1)} %fusion, bf16[1024,2048]{1,0:T(8,128)(2,1)S(1)} %copy-done.11, bf16[2048,896]{1,0:T(8,128)(2,1)S(1)} %copy-done.12), kind=kOutput, calls=%fused_computation | convolution fusion | flops 3759013888 | bytes 15204352 | tf_op jit(solution)/shard_map/dot_general | solution.py:31
  195.3 0.9 shard_map.56.own_ref
  196.2 2.5 %collective-permute-start.23 = (bf16[1024,512]{1,0:T(8,128)(2,1)S(1)}, bf16[1024,512]{1,0:T(8,128)(2,1)S(1)}, u32[]{:S(2)}, u32[]{:S(2)}) collective-permute-start(bf16[1024,512]{1,0:T(8,128)(2,1)S(1)} %shard_map.56.own_ref), channel_id=1, source_target_pairs={{0,1},{1,0},{2,3},{3,2},{4,5},{5,4},{6,7},{7,6},{8,9},{9,8},{10,11... | collective-permute-start | bytes 3145736 | tf_op jit(solution)/shard_map/ppermute | solution.py:23
  198.8 2.3 %collective-permute-done.23.other_ref = bf16[1024,512]{1,0:T(8,128)(2,1)S(1)} collective-permute-done((bf16[1024,512]{1,0:T(8,128)(2,1)S(1)}, bf16[1024,512]{1,0:T(8,128)(2,1)S(1)}, u32[]{:S(2)}, u32[]{:S(2)}) %collective-permute-start.23) | collective-permute-done | bytes 1048608 | tf_op jit(solution)/shard_map/ppermute | solution.py:23
  201.1 17.8 %shard_map.57 = f32[1024,896]{1,0:T(8,128)} custom-call(f32[1024,896]{1,0:T(8,128)} %convolution_add_fusion.rest_4_.g_ref, f32[1024,512]{1,0:T(8,128)} %u_ref.5, bf16[512,896]{1,0:T(8,128)(2,1)S(1)} %bitcast.19, bf16[1024,512]{1,0:T(8,128)(2,1)S(1)} %shard_map.56.own_ref, bf16[1024,512]{1,0:T(8,128)(2,1)S(1)} %collective-permute-done.23.other_ref, ...), custom_call_target="tpu_custom_call" | custom-call | flops 8455716864 | bytes 16777216 | tf_op jit(solution)/shard_map/pallas_call | solution.py:321
  (53 shorter events, 0.9 us)
Async XLA Ops:
  0.1 1.0 copy-start.6
  6.8 11.5 %copy-start.7 = (bf16[128,1024]{1,0:T(8,128)(2,1)S(1)}, bf16[128,1024]{1,0:T(8,128)(2,1)}, u32[]{:S(2)}) copy-start(bf16[128,1024]{1,0:T(8,128)(2,1)} %a_ref.1) | copy-start | bytes 786436
  6.8 6.0 %collective-permute-start = (f32[512,512]{1,0:T(8,128)S(1)}, f32[512,512]{1,0:T(8,128)S(1)}, u32[]{:S(2)}, u32[]{:S(2)}) collective-permute-start(f32[512,512]{1,0:T(8,128)S(1)} %get-tuple-element.27), channel_id=1, source_target_pairs={{0,1},{1,0},{2,3},{3,2},{4,5},{5,4},{6,7},{7,6},{8,9},{9,8},{10,11... | collective-permute-start | bytes 3145736 | tf_op jit(solution)/shard_map/ppermute | solution.py:23
  10.1 24.3 %collective-permute-start.1 = (bf16[512,896]{1,0:T(8,128)(2,1)}, bf16[512,896]{1,0:T(8,128)(2,1)S(1)}, u32[]{:S(2)}, u32[]{:S(2)}) collective-permute-start(bf16[512,896]{1,0:T(8,128)(2,1)} %rest_0_.1), channel_id=1, source_target_pairs={{0,64},{64,128},{128,192},{192,0},{1,65},{65,129},{129,193},{193,1... | collective-permute-start | bytes 2752520 | tf_op jit(solution)/shard_map/ppermute | solution.py:23
  10.1 24.3 %collective-permute-start.2 = (bf16[512,896]{1,0:T(8,128)(2,1)}, bf16[512,896]{1,0:T(8,128)(2,1)S(1)}, u32[]{:S(2)}, u32[]{:S(2)}) collective-permute-start(bf16[512,896]{1,0:T(8,128)(2,1)} %rest_0_.1), channel_id=1, source_target_pairs={{0,192},{64,0},{128,64},{192,128},{1,193},{65,1},{129,65},{193,129... | collective-permute-start | bytes 2752520 | tf_op jit(solution)/shard_map/ppermute | solution.py:23
  12.8 21.6 %collective-permute-start.3 = (bf16[512,896]{1,0:T(8,128)(2,1)}, bf16[512,896]{1,0:T(8,128)(2,1)S(1)}, u32[]{:S(2)}, u32[]{:S(2)}) collective-permute-start(bf16[512,896]{1,0:T(8,128)(2,1)} %rest_0_.1), channel_id=1, source_target_pairs={{0,32},{32,0},{1,33},{33,1},{2,34},{34,2},{3,35},{35,3},{4,36},{36... | collective-permute-start | bytes 2752520 | tf_op jit(solution)/shard_map/ppermute | solution.py:23
  14.0 18.4 %all-to-all-start = ((f32[4,128,512]{2,1,0:T(8,128)}), f32[4,128,512]{2,1,0:T(8,128)}, u32[]{:S(2)}, u32[]{:S(2)}) async-start(f32[4,128,512]{2,1,0:T(8,128)} %bitcast.23), calls=%async_computation | async-start | bytes 2097152 | tf_op jit(solution)/shard_map/all_to_all | solution.py:343
  34.4 64.4 %copy-start = (bf16[512,896]{1,0:T(8,128)(2,1)}, bf16[512,896]{1,0:T(8,128)(2,1)S(1)}, u32[]{:S(2)}) copy-start(bf16[512,896]{1,0:T(8,128)(2,1)S(1)} %collective-permute-done.2.right.rest_3_) | copy-start | bytes 2752516
  37.1 9.8 %copy-start.8 = (bf16[1024,128]{1,0:T(8,128)(2,1)}, bf16[1024,128]{1,0:T(8,128)(2,1)S(1)}, u32[]{:S(2)}) copy-start(bf16[1024,128]{1,0:T(8,128)(2,1)S(1)} %get-tuple-element.34.a) | copy-start | bytes 786436
  46.9 14.8 %all-to-all-start.1 = ((f32[4,32,512]{2,1,0:T(8,128)}), f32[4,32,512]{2,1,0:T(8,128)S(1)}, u32[]{:S(2)}, u32[]{:S(2)}) async-start(f32[4,32,512]{2,1,0:T(8,128)} %bitcast.6), calls=%async_computation.1 | async-start | bytes 524288 | tf_op jit(solution)/shard_map/all_to_all | solution.py:353
  53.6 51.2 %collective-permute-start.6 = (bf16[768,896]{1,0:T(8,128)(2,1)}, bf16[768,896]{1,0:T(8,128)(2,1)}, u32[]{:S(2)}, u32[]{:S(2)}) collective-permute-start(bf16[768,896]{1,0:T(8,128)(2,1)} %get-tuple-element.32), channel_id=1, source_target_pairs={{0,64},{64,128},{128,192},{192,0},{1,65},{65,129},{129,193},{193,1... | collective-permute-start | bytes 4128776 | tf_op jit(solution)/shard_map/ppermute | solution.py:23
  53.6 51.2 %collective-permute-start.7 = (bf16[768,896]{1,0:T(8,128)(2,1)}, bf16[768,896]{1,0:T(8,128)(2,1)}, u32[]{:S(2)}, u32[]{:S(2)}) collective-permute-start(bf16[768,896]{1,0:T(8,128)(2,1)} %get-tuple-element.33), channel_id=1, source_target_pairs={{0,192},{64,0},{128,64},{192,128},{1,193},{65,1},{129,65},{193,129... | collective-permute-start | bytes 4128776 | tf_op jit(solution)/shard_map/ppermute | solution.py:23
  61.6 0.9 copy-start.13
  62.6 35.4 %all-to-all-start.4 = ((f32[16,64,128]{2,1,0:T(8,128)}), f32[16,64,128]{2,1,0:T(8,128)S(1)}, u32[]{:S(2)}, u32[]{:S(2)}) async-start(f32[16,64,128]{2,1,0:T(8,128)} %broadcast_in_dim.10), calls=%async_computation.4 | async-start | bytes 1048576 | tf_op jit(solution)/shard_map/all_to_all | solution.py:27
  67.4 37.4 %collective-permute-start.8 = (bf16[1024,128]{1,0:T(8,128)(2,1)}, bf16[1024,128]{1,0:T(8,128)(2,1)}, u32[]{:S(2)}, u32[]{:S(2)}) collective-permute-start(bf16[1024,128]{1,0:T(8,128)(2,1)} %copy-done.8), channel_id=1, source_target_pairs={{0,2},{2,4},{4,6},{6,0},{1,3},{3,5},{5,7},{7,1},{8,10},{10,12},{12... | collective-permute-start | bytes 786440 | tf_op jit(solution)/shard_map/ppermute | solution.py:23
  69.6 35.2 %collective-permute-start.9 = (bf16[1024,128]{1,0:T(8,128)(2,1)}, bf16[1024,128]{1,0:T(8,128)(2,1)}, u32[]{:S(2)}, u32[]{:S(2)}) collective-permute-start(bf16[1024,128]{1,0:T(8,128)(2,1)} %copy-done.8), channel_id=1, source_target_pairs={{0,6},{2,0},{4,2},{6,4},{1,7},{3,1},{5,3},{7,5},{8,14},{10,8},{12,... | collective-permute-start | bytes 786440 | tf_op jit(solution)/shard_map/ppermute | solution.py:23
  71.0 33.8 %collective-permute-start.10 = (bf16[1024,128]{1,0:T(8,128)(2,1)}, bf16[1024,128]{1,0:T(8,128)(2,1)}, u32[]{:S(2)}, u32[]{:S(2)}) collective-permute-start(bf16[1024,128]{1,0:T(8,128)(2,1)} %copy-done.8), channel_id=1, source_target_pairs={{0,4},{2,6},{4,0},{6,2},{1,5},{3,7},{5,1},{7,3},{8,12},{10,14},{12... | collective-permute-start | bytes 786440 | tf_op jit(solution)/shard_map/ppermute | solution.py:23
  98.8 16.9 %all-to-all-start.2 = ((f32[8,32,512]{2,1,0:T(8,128)}), f32[8,32,512]{2,1,0:T(8,128)S(1)}, u32[]{:S(2)}, u32[]{:S(2)}) async-start(f32[8,32,512]{2,1,0:T(8,128)} %broadcast_in_dim.9), calls=%async_computation.2 | async-start | bytes 1048576 | tf_op jit(solution)/shard_map/all_to_all | solution.py:27
  104.8 1.0 copy-start.9
  108.5 39.2 %collective-permute-start.11 = (bf16[4,1024,128]{2,1,0:T(8,128)(2,1)}, bf16[4,1024,128]{2,1,0:T(8,128)(2,1)}, u32[]{:S(2)}, u32[]{:S(2)}) collective-permute-start(bf16[4,1024,128]{2,1,0:T(8,128)(2,1)} %get-tuple-element.35.rest_0_), channel_id=1, source_target_pairs={{0,8},{8,16},{16,24},{24,0},{1,9},{9,17},{17,25},{25,1},{2,10},{10... | collective-permute-start | bytes 3145736 | tf_op jit(solution)/shard_map/ppermute | solution.py:23
  109.5 38.2 %collective-permute-start.12 = (bf16[4,1024,128]{2,1,0:T(8,128)(2,1)}, bf16[4,1024,128]{2,1,0:T(8,128)(2,1)}, u32[]{:S(2)}, u32[]{:S(2)}) collective-permute-start(bf16[4,1024,128]{2,1,0:T(8,128)(2,1)} %get-tuple-element.35.rest_0_), channel_id=1, source_target_pairs={{0,24},{8,0},{16,8},{24,16},{1,25},{9,1},{17,9},{25,17},{2,26},{10... | collective-permute-start | bytes 3145736 | tf_op jit(solution)/shard_map/ppermute | solution.py:23
  111.3 45.4 %collective-permute-start.13 = (bf16[4,1024,128]{2,1,0:T(8,128)(2,1)}, bf16[4,1024,128]{2,1,0:T(8,128)(2,1)}, u32[]{:S(2)}, u32[]{:S(2)}) collective-permute-start(bf16[4,1024,128]{2,1,0:T(8,128)(2,1)} %get-tuple-element.35.rest_0_), channel_id=1, source_target_pairs={{0,16},{8,24},{16,0},{24,8},{1,17},{9,25},{17,1},{25,9},{2,18},{10... | collective-permute-start | bytes 3145736 | tf_op jit(solution)/shard_map/ppermute | solution.py:23
  112.5 26.2 %collective-permute-start.14 = (bf16[512,896]{1,0:T(8,128)(2,1)}, bf16[512,896]{1,0:T(8,128)(2,1)}, u32[]{:S(2)}, u32[]{:S(2)}) collective-permute-start(bf16[512,896]{1,0:T(8,128)(2,1)} %get-tuple-element.39), channel_id=1, source_target_pairs={{0,32},{32,0},{1,33},{33,1},{2,34},{34,2},{3,35},{35,3},{4,36},{36... | collective-permute-start | bytes 2752520 | tf_op jit(solution)/shard_map/ppermute | solution.py:23
  113.2 4.2 %collective-permute-start.4 = (f32[16,64,128]{2,1,0:T(8,128)S(1)}, f32[16,64,128]{2,1,0:T(8,128)}, u32[]{:S(2)}, u32[]{:S(2)}) collective-permute-start(f32[16,64,128]{2,1,0:T(8,128)S(1)} %all-to-all-done.4.own_ref), channel_id=1, source_target_pairs={{0,1},{1,0},{2,3},{3,2},{4,5},{5,4},{6,7},{7,6},{8,9},{9,8},{10,11... | collective-permute-start | bytes 1572872 | tf_op jit(solution)/shard_map/ppermute | solution.py:23
  119.2 1.0 copy-start.3
  120.2 27.5 %collective-permute-start.5 = (f32[32,2048]{1,0:T(8,128)S(1)}, f32[32,2048]{1,0:T(8,128)S(1)}, u32[]{:S(2)}, u32[]{:S(2)}) collective-permute-start(f32[32,2048]{1,0:T(8,128)S(1)} %get-tuple-element.31), channel_id=1, source_target_pairs={{0,1},{1,0},{2,3},{3,2},{4,5},{5,4},{6,7},{7,6},{8,9},{9,8},{10,11... | collective-permute-start | bytes 786440 | tf_op jit(solution)/shard_map/ppermute | solution.py:23
  121.3 13.2 %all-to-all-start.5 = ((f32[8,1,2048]{2,1,0:T(1,128)}), f32[8,1,2048]{2,1,0:T(1,128)S(1)}, u32[]{:S(2)}, u32[]{:S(2)}) async-start(f32[8,1,2048]{2,1,0:T(1,128)} %reshape.16), calls=%async_computation.5 | async-start | bytes 131072 | tf_op jit(solution)/shard_map/all_to_all | solution.py:27
  128.2 1.3 copy-start.2
  129.4 1.3 copy-start.10
  136.0 1.6 copy-start.1
  161.5 3.2 %collective-permute-start.15 = (f32[32,1024]{1,0:T(8,128)S(1)}, f32[32,1024]{1,0:T(8,128)S(1)}, u32[]{:S(2)}, u32[]{:S(2)}) collective-permute-start(f32[32,1024]{1,0:T(8,128)S(1)} %get-tuple-element.43), channel_id=1, source_target_pairs={{0,1},{1,0},{2,3},{3,2},{4,5},{5,4},{6,7},{7,6},{8,9},{9,8},{10,11... | collective-permute-start | bytes 393224 | tf_op jit(solution)/shard_map/ppermute | solution.py:23
  164.7 0.6 copy-start.4
  165.3 0.8 copy-start.5
  165.4 16.1 %collective-permute-start.16 = (bf16[1024,2048]{1,0:T(8,128)(2,1)}, bf16[1024,2048]{1,0:T(8,128)(2,1)}, u32[]{:S(2)}, u32[]{:S(2)}) collective-permute-start(bf16[1024,2048]{1,0:T(8,128)(2,1)} %shard_map.55), channel_id=1, source_target_pairs={{0,1},{1,0},{2,3},{3,2},{4,5},{5,4},{6,7},{7,6},{8,9},{9,8},{10,11... | collective-permute-start | bytes 12582920 | tf_op jit(solution)/shard_map/ppermute | solution.py:23
  166.2 10.5 %collective-permute-start.19 = (bf16[32,1024]{1,0:T(8,128)(2,1)S(1)}, bf16[32,1024]{1,0:T(8,128)(2,1)S(1)}, u32[]{:S(2)}, u32[]{:S(2)}) collective-permute-start(bf16[32,1024]{1,0:T(8,128)(2,1)S(1)} %copy-done.5), channel_id=1, source_target_pairs={{0,4},{2,6},{4,0},{6,2},{1,5},{3,7},{5,1},{7,3},{8,12},{10,14},{12... | collective-permute-start | bytes 196616 | tf_op jit(solution)/shard_map/ppermute | solution.py:23
  169.5 8.0 %collective-permute-start.18 = (bf16[32,1024]{1,0:T(8,128)(2,1)S(1)}, bf16[32,1024]{1,0:T(8,128)(2,1)S(1)}, u32[]{:S(2)}, u32[]{:S(2)}) collective-permute-start(bf16[32,1024]{1,0:T(8,128)(2,1)S(1)} %copy-done.5), channel_id=1, source_target_pairs={{0,6},{2,0},{4,2},{6,4},{1,7},{3,1},{5,3},{7,5},{8,14},{10,8},{12,... | collective-permute-start | bytes 196616 | tf_op jit(solution)/shard_map/ppermute | solution.py:23
  172.8 5.8 %collective-permute-start.17 = (bf16[32,1024]{1,0:T(8,128)(2,1)S(1)}, bf16[32,1024]{1,0:T(8,128)(2,1)S(1)}, u32[]{:S(2)}, u32[]{:S(2)}) collective-permute-start(bf16[32,1024]{1,0:T(8,128)(2,1)S(1)} %copy-done.5), channel_id=1, source_target_pairs={{0,2},{2,4},{4,6},{6,0},{1,3},{3,5},{5,7},{7,1},{8,10},{10,12},{12... | collective-permute-start | bytes 196616 | tf_op jit(solution)/shard_map/ppermute | solution.py:23
  172.8 22.5 %all-to-all-start.6 = ((bf16[8,64,896]{2,1,0:T(8,128)(2,1)}), bf16[8,64,896]{2,1,0:T(8,128)(2,1)S(1)}, u32[]{:S(2)}, u32[]{:S(2)}) async-start(bf16[8,64,896]{2,1,0:T(8,128)(2,1)} %get-tuple-element.45), calls=%async_computation.6 | async-start | bytes 1835008 | tf_op jit(solution)/shard_map/all_to_all | solution.py:368
  178.7 16.6 %collective-permute-start.20 = (bf16[4,32,1024]{2,1,0:T(8,128)(2,1)S(1)}, bf16[4,32,1024]{2,1,0:T(8,128)(2,1)S(1)}, u32[]{:S(2)}, u32[]{:S(2)}) collective-permute-start(bf16[4,32,1024]{2,1,0:T(8,128)(2,1)S(1)} %pad_maximum_fusion.rest_0_), channel_id=1, source_target_pairs={{0,8},{8,16},{16,24},{24,0},{1,9},{9,17},{17,25},{25,1},{2,10},{10... | collective-permute-start | bytes 786440 | tf_op jit(solution)/shard_map/ppermute | solution.py:23
  179.5 15.8 %collective-permute-start.21 = (bf16[4,32,1024]{2,1,0:T(8,128)(2,1)S(1)}, bf16[4,32,1024]{2,1,0:T(8,128)(2,1)S(1)}, u32[]{:S(2)}, u32[]{:S(2)}) collective-permute-start(bf16[4,32,1024]{2,1,0:T(8,128)(2,1)S(1)} %pad_maximum_fusion.rest_0_), channel_id=1, source_target_pairs={{0,24},{8,0},{16,8},{24,16},{1,25},{9,1},{17,9},{25,17},{2,26},{10... | collective-permute-start | bytes 786440 | tf_op jit(solution)/shard_map/ppermute | solution.py:23
  181.4 13.9 %collective-permute-start.22 = (bf16[4,32,1024]{2,1,0:T(8,128)(2,1)S(1)}, bf16[4,32,1024]{2,1,0:T(8,128)(2,1)S(1)}, u32[]{:S(2)}, u32[]{:S(2)}) collective-permute-start(bf16[4,32,1024]{2,1,0:T(8,128)(2,1)S(1)} %pad_maximum_fusion.rest_0_), channel_id=1, source_target_pairs={{0,16},{8,24},{16,0},{24,8},{1,17},{9,25},{17,1},{25,9},{2,18},{10... | collective-permute-start | bytes 786440 | tf_op jit(solution)/shard_map/ppermute | solution.py:23
  181.4 7.5 %copy-start.11 = (bf16[1024,2048]{1,0:T(8,128)(2,1)S(1)}, bf16[1024,2048]{1,0:T(8,128)(2,1)}, u32[]{:S(2)}) copy-start(bf16[1024,2048]{1,0:T(8,128)(2,1)} %shard_map.55) | copy-start | bytes 12582916
  181.4 7.5 %copy-start.12 = (bf16[2048,896]{1,0:T(8,128)(2,1)S(1)}, bf16[2048,896]{1,0:T(8,128)(2,1)}, u32[]{:S(2)}) copy-start(bf16[2048,896]{1,0:T(8,128)(2,1)} %get-tuple-element.40.rest_6_) | copy-start | bytes 11010052
  196.2 4.8 %collective-permute-start.23 = (bf16[1024,512]{1,0:T(8,128)(2,1)S(1)}, bf16[1024,512]{1,0:T(8,128)(2,1)S(1)}, u32[]{:S(2)}, u32[]{:S(2)}) collective-permute-start(bf16[1024,512]{1,0:T(8,128)(2,1)S(1)} %shard_map.56.own_ref), channel_id=1, source_target_pairs={{0,1},{1,0},{2,3},{3,2},{4,5},{5,4},{6,7},{7,6},{8,9},{9,8},{10,11... | collective-permute-start | bytes 3145736 | tf_op jit(solution)/shard_map/ppermute | solution.py:23

commit v2 on v1

--- a/solution.py
+++ b/solution.py
@@ -49,8 +49,8 @@
 
 def decode(code):
     wide = code.astype(F32)
-    root = jnp.sqrt(jnp.sqrt(jnp.abs(wide)))
-    return jnp.where(wide < 0, -root, root)
+    root = lax.rsqrt(lax.rsqrt(jnp.abs(wide)))
+    return jnp.where(wide < 0, -root, jnp.where(wide > 0, root, 0.0))
 
 
 def call(kernel, out_shape, in_specs, scratch=(), flops=0, moved=0, **extra):
@@ -90,7 +90,8 @@
     )(at, a, c, u, v)
 
 
-def prepare_kernel(at, v_ref, high_ref, low_ref):
+def prepare_kernel(at, v_ref, u_ref, high_ref, low_ref, uh_ref, ul_ref):
+    uh_ref[...], ul_ref[...] = split(u_ref[...])
     for n, which in enumerate((at[C], 1 - at[C])):
         turned = v_ref[:, pl.ds(pl.multiple_of(which * 512, 512), 512)].T
         high, low = split(turned)
@@ -98,10 +99,9 @@
         low_ref[512 * n : 512 * n + 512, :] = low
 
 
-def prepare(at, v):
-    return call(
-        prepare_kernel, (shape(1024, 896, kind=BF16), shape(1024, 896, kind=BF16)), [SMEM, VMEM], moved=8 << 20
-    )(at, v)
+def prepare(at, v, u):
+    tall, wide = shape(1024, 896, kind=BF16), shape(1024, 512, kind=BF16)
+    return call(prepare_kernel, (tall, tall, wide, wide), [SMEM, VMEM, VMEM], moved=12 << 20)(at, v, u)
 
 
 def run(copies, sems):
@@ -296,7 +296,7 @@
     )(at, p2, *pieces)
 
 
-def final_kernel(g_ref, u_ref, r_ref, own_ref, other_ref, high_ref, low_ref, out_ref, rh_ref, rl_ref):
+def final_kernel(g_ref, uh_ref, ul_ref, r_ref, own_ref, other_ref, high_ref, low_ref, out_ref, rh_ref, rl_ref):
     @pl.when(pl.program_id(0) == 0)
     def _():
         high, low = split(decode(r_ref[...]))
@@ -305,13 +305,14 @@
         rh_ref[512:, :] = high_ref[...]
         rl_ref[512:, :] = low_ref[...]
 
-    parts = [u_ref[...], decode(own_ref[...]), decode(other_ref[...])]
-    highs, lows = zip(*map(split, parts))
-    high, low = jnp.concatenate(highs, axis=1), jnp.concatenate(lows, axis=1)
+    own_high, own_low = split(decode(own_ref[...]))
+    other_high, other_low = split(decode(other_ref[...]))
+    high = jnp.concatenate([uh_ref[...], own_high, other_high], axis=1)
+    low = jnp.concatenate([ul_ref[...], own_low, other_low], axis=1)
     out_ref[...] = g_ref[...] - (dot(high, rh_ref[...]) + (dot(high, rl_ref[...]) + dot(low, rh_ref[...])))
 
 
-def final(g, u, r, own, other, high, low):
+def final(g, uh, ul, r, own, other, high, low):
     def rows(width):
         return pl.BlockSpec((512, width), lambda k: (k, 0))
 
@@ -321,13 +322,13 @@
     return pl.pallas_call(
         final_kernel,
         grid=(2,),
-        in_specs=[rows(896), rows(512), whole(512), rows(512), rows(512), whole(1024), whole(1024)],
+        in_specs=[rows(896), rows(512), rows(512), whole(512), rows(512), rows(512), whole(1024), whole(1024)],
         out_specs=rows(896),
         out_shape=shape(1024, 896),
         scratch_shapes=[pltpu.VMEM((1536, 896), BF16)] * 2,
         compiler_params=pltpu.CompilerParams(vmem_limit_bytes=50 << 20),
         cost_estimate=pl.CostEstimate(flops=6 * 1024 * 896 * 1536, bytes_accessed=16 << 20, transcendentals=0),
-    )(g, u, r, own, other, high, low)
+    )(g, uh, ul, r, own, other, high, low)
 
 
 def add_up(parts):
@@ -363,7 +364,7 @@
     here, there, p2, t = coefficients(at, q, p_own, shift(p_own, "c", 1))
     there = shift(there, "c", 1)
     taken = cross(spread(t, IN, 8), u)
-    vh, vl = prepare(at, v)
+    vh, vl, uh, ul = prepare(at, v, u)
     r, c_own, c_other = r_slices(at, p2, (c, mate, left, right, xp, xm, far))
     r = lax.all_to_all(r, IN, 0, 0).reshape(512, 896)
 
@@ -374,7 +375,7 @@
     spieces = [column] + [shift(column, "y", step) for step in (1, -1, 2)]
     g = dot(a_own, c_own) + dot(shift(a_own, "c", 1), c_other)
     s = turn(at, spieces, (g, r))
-    return final(g, u, r, s, shift(s, "c", 1), vh, vl)
+    return final(g, uh, ul, r, s, shift(s, "c", 1), vh, vl)
 
 
 def solution(mesh):

time: 220 us -> 219 us (level)
    all_to_all x3, waiting for transfers between devices: 24.6 us -> 22.2 us  [spread(): lax.all_to_all(jnp.broadcast_to(value, (count,) + value.shape), axes, 0, 0)]
    unnamed x31 -> x43, local copies, waits for them, and re-layouts: 9.11 us -> 10.3 us
  transfers between devices with their start and end apart: 30 -> 30, of which waited for: 10 -> 10; matrix products, arithmetic and copies ran while one was open for 11% -> 11% of each run, Pallas kernels for 8% -> 9%
where the time goes in v2:
time: 219 us; the launch traced here: 218 us
  starting transfers between devices  69.1 us (32%)
  waiting for transfers between devices  56.8 us (26%)
  Pallas kernels  49.8 us (23%)
  matrix products  13.8 us (6%)
  local copies, waits for them, and re-layouts  12.7 us (6%)
  blocking collectives  9.76 us (4%)
  other arithmetic  5.91 us (3%)
    ppermute x24, starting transfers between devices, shift(): lax.ppermute(value, axis, [(k, (k + step) % size) for k in range(size)])  39.6 us
    all_to_all x3, waiting for transfers between devices, spread(): lax.all_to_all(jnp.broadcast_to(value, (count,) + value.shape), axes, 0, 0)  22.2 us
    ppermute x24, waiting for transfers between devices, shift(): lax.ppermute(value, axis, [(k, (k + step) % size) for k in range(size)])  16.3 us
    pallas_call x1, Pallas kernels, final(): pl.pallas_call(final_kernel, grid=(2,), in_specs=[rows(896), rows(512), r...  15.6 us
    all_to_all x3, starting transfers between devices, spread(): lax.all_to_all(jnp.broadcast_to(value, (count,) + value.shape), axes, 0, 0)  14.6 us
    all_to_all x1, waiting for transfers between devices, per_device(): q = add_up(lax.all_to_all(q.reshape(4, 128, 512), 'y', 0, 0))  13.9 us
    dot_general x2, matrix products, dot(): lax.dot_general(left, right, (dims, ((), ())), preferred_element_type=F32)  13.8 us
    unnamed x43, local copies, waits for them, and re-layouts  10.3 us
  transfers between devices with their start and end apart: 30, of which 10 were waited for; matrix products, arithmetic and copies ran while one was open for 11% of the time, Pallas kernels for 9%

profile of v2, /device:TPU:1, one launch (start us, length us, event | category | flops | bytes accessed | tf_op | source)
XLA Modules:
  0.0 218.2 jit_solution(1782764567962461039)
XLA Ops:
  0.1 0.9 copy-done.8
  1.0 5.8 %shard_map.46 = (f32[512,128]{1,0:T(8,128)S(1)}, f32[512,512]{1,0:T(8,128)S(1)}, f32[512,512]{1,0:T(8,128)S(1)}) custom-call(s32[5]{0:T(128)S(1)} %stack.38.at, bf16[128,1024]{1,0:T(8,128)(2,1)S(1)} %copy-done.8, bf16[512,896]{1,0:T(8,128)(2,1)} %rest_0_.1, f32[1024,512]{1,0:T(8,128)} %u_ref.5, f32[896,1024]{1,0:T(8,128)} %v_ref.3), custom_call_target="tpu_custom_call" | custom-call | flops 2147483648 | bytes 10485760 | tf_op jit(solution)/shard_map/pallas_call | solution.py:84
  6.8 3.3 %collective-permute-start = (f32[512,512]{1,0:T(8,128)S(1)}, f32[512,512]{1,0:T(8,128)S(1)}, u32[]{:S(2)}, u32[]{:S(2)}) collective-permute-start(f32[512,512]{1,0:T(8,128)S(1)} %get-tuple-element.29), channel_id=1, source_target_pairs={{0,1},{1,0},{2,3},{3,2},{4,5},{5,4},{6,7},{7,6},{8,9},{9,8},{10,11... | collective-permute-start | bytes 3145736 | tf_op jit(solution)/shard_map/ppermute | solution.py:23
  10.2 2.7 %collective-permute-start.2 = (bf16[512,896]{1,0:T(8,128)(2,1)}, bf16[512,896]{1,0:T(8,128)(2,1)S(1)}, u32[]{:S(2)}, u32[]{:S(2)}) collective-permute-start(bf16[512,896]{1,0:T(8,128)(2,1)} %rest_0_.1), channel_id=1, source_target_pairs={{0,192},{64,0},{128,64},{192,128},{1,193},{65,1},{129,65},{193,129... | collective-permute-start | bytes 2752520 | tf_op jit(solution)/shard_map/ppermute | solution.py:23
  12.9 1.2 add.6
  14.0 4.2 %all-to-all-start = ((f32[4,128,512]{2,1,0:T(8,128)}), f32[4,128,512]{2,1,0:T(8,128)}, u32[]{:S(2)}, u32[]{:S(2)}) async-start(f32[4,128,512]{2,1,0:T(8,128)} %bitcast.23), calls=%async_computation | async-start | bytes 2097152 | tf_op jit(solution)/shard_map/all_to_all | solution.py:344
  18.5 13.9 %all-to-all-done = f32[4,128,512]{2,1,0:T(8,128)} async-done(((f32[4,128,512]{2,1,0:T(8,128)}), f32[4,128,512]{2,1,0:T(8,128)}, u32[]{:S(2)}, u32[]{:S(2)}) %all-to-all-start) | async-done | bytes 1048608 | tf_op jit(solution)/shard_map/all_to_all | solution.py:344
  32.4 2.0 reduce_sum.27.rest_0_
  34.5 2.6 %shard_map.47 = (bf16[768,896]{1,0:T(8,128)(2,1)}, bf16[768,896]{1,0:T(8,128)(2,1)}, bf16[1024,128]{1,0:T(8,128)(2,1)S(1)}, f32[512,128]{1,0:T(8,128)S(1)}) custom-call(bf16[512,896]{1,0:T(8,128)(2,1)S(1)} %collective-permute-done.1.left.rest_2_, bf16[512,896]{1,0:T(8,128)(2,1)S(1)} %collective-permute-done.2.right.rest_3_, ...), custom_call_target="tpu_custom_call" | custom-call | bytes 8388608 | tf_op jit(solution)/shard_map/pallas_call | solution.py:141
  37.1 9.8 %all_to_all.35 = f32[8,64,128]{2,1,0:T(8,128)} all-to-all(f32[8,64,128]{2,1,0:T(8,128)S(1)} %bitcast.22), channel_id=1, replica_groups=mesh['x'=4,'l'=2,'y'=4,'h'=4,'c'=2] {'x','l'}, dimensions={0} | all-to-all | bytes 524288 | tf_op jit(solution)/shard_map/all_to_all | solution.py:353
  46.9 6.8 %all-to-all-start.1 = ((f32[4,32,512]{2,1,0:T(8,128)}), f32[4,32,512]{2,1,0:T(8,128)S(1)}, u32[]{:S(2)}, u32[]{:S(2)}) async-start(f32[4,32,512]{2,1,0:T(8,128)} %bitcast.6), calls=%async_computation.1 | async-start | bytes 524288 | tf_op jit(solution)/shard_map/all_to_all | solution.py:354
  53.7 2.7 %collective-permute-start.7 = (bf16[768,896]{1,0:T(8,128)(2,1)}, bf16[768,896]{1,0:T(8,128)(2,1)}, u32[]{:S(2)}, u32[]{:S(2)}) collective-permute-start(bf16[768,896]{1,0:T(8,128)(2,1)} %get-tuple-element.35), channel_id=1, source_target_pairs={{0,192},{64,0},{128,64},{192,128},{1,193},{65,1},{129,65},{193,129... | collective-permute-start | bytes 4128776 | tf_op jit(solution)/shard_map/ppermute | solution.py:23
  56.3 1.0 reduce_sum.29.rest_1_
  57.3 4.4 %all-to-all-done.1 = f32[4,32,512]{2,1,0:T(8,128)S(1)} async-done(((f32[4,32,512]{2,1,0:T(8,128)}), f32[4,32,512]{2,1,0:T(8,128)S(1)}, u32[]{:S(2)}, u32[]{:S(2)}) %all-to-all-start.1) | async-done | bytes 262176 | tf_op jit(solution)/shard_map/all_to_all | solution.py:354
  61.7 0.9 broadcast_in_dim.10
  62.6 4.8 %all-to-all-start.4 = ((f32[16,64,128]{2,1,0:T(8,128)}), f32[16,64,128]{2,1,0:T(8,128)S(1)}, u32[]{:S(2)}, u32[]{:S(2)}) async-start(f32[16,64,128]{2,1,0:T(8,128)} %broadcast_in_dim.10), calls=%async_computation.4 | async-start | bytes 1048576 | tf_op jit(solution)/shard_map/all_to_all | solution.py:27
  67.4 2.3 %collective-permute-start.8 = (bf16[1024,128]{1,0:T(8,128)(2,1)}, bf16[1024,128]{1,0:T(8,128)(2,1)}, u32[]{:S(2)}, u32[]{:S(2)}) collective-permute-start(bf16[1024,128]{1,0:T(8,128)(2,1)} %copy-done.10), channel_id=1, source_target_pairs={{0,2},{2,4},{4,6},{6,0},{1,3},{3,5},{5,7},{7,1},{8,10},{10,12},{12... | collective-permute-start | bytes 786440 | tf_op jit(solution)/shard_map/ppermute | solution.py:23
  69.6 1.4 collective-permute-start.9
  71.0 5.2 %collective-permute-start.10 = (bf16[1024,128]{1,0:T(8,128)(2,1)}, bf16[1024,128]{1,0:T(8,128)(2,1)}, u32[]{:S(2)}, u32[]{:S(2)}) collective-permute-start(bf16[1024,128]{1,0:T(8,128)(2,1)} %copy-done.10), channel_id=1, source_target_pairs={{0,4},{2,6},{4,0},{6,2},{1,5},{3,7},{5,1},{7,3},{8,12},{10,14},{12... | collective-permute-start | bytes 786440 | tf_op jit(solution)/shard_map/ppermute | solution.py:23
  76.2 1.0 reduce_sum.28.rest_0_
  77.2 20.8 %all-to-all-done.4.own_ref = f32[16,64,128]{2,1,0:T(8,128)S(1)} async-done(((f32[16,64,128]{2,1,0:T(8,128)}), f32[16,64,128]{2,1,0:T(8,128)S(1)}, u32[]{:S(2)}, u32[]{:S(2)}) %all-to-all-start.4) | async-done | bytes 524320 | tf_op jit(solution)/shard_map/all_to_all | solution.py:27
  98.0 0.9 broadcast_in_dim.9
  98.8 6.0 %all-to-all-start.2 = ((f32[8,32,512]{2,1,0:T(8,128)}), f32[8,32,512]{2,1,0:T(8,128)S(1)}, u32[]{:S(2)}, u32[]{:S(2)}) async-start(f32[8,32,512]{2,1,0:T(8,128)} %broadcast_in_dim.9), calls=%async_computation.2 | async-start | bytes 1048576 | tf_op jit(solution)/shard_map/all_to_all | solution.py:27
  104.9 0.9 copy-done.11
  105.8 2.7 %shard_map.49 = (bf16[512,896]{1,0:T(8,128)(2,1)}, bf16[4,1024,128]{2,1,0:T(8,128)(2,1)}) custom-call(bf16[768,896]{1,0:T(8,128)(2,1)} %collective-permute-done.6.xp.rest_4_, bf16[768,896]{1,0:T(8,128)(2,1)} %collective-permute-done.7.xm.rest_5_, bf16[1024,128]{1,0:T(8,128)(2,1)S(1)} %copy-done.11, bf16[1024,128]{1,0:T(8,128)(2,1)} %collective-permute-done.8.hp, ...), custom_call_target="tpu_custom_call" | custom-call | bytes 8388608 | tf_op jit(solution)/shard_map/pallas_call | solution.py:141
  108.6 1.0 collective-permute-start.11
  109.5 1.8 collective-permute-start.12
  111.3 1.2 collective-permute-start.13
  112.5 0.7 collective-permute-start.14
  113.3 2.5 %collective-permute-start.4 = (f32[16,64,128]{2,1,0:T(8,128)S(1)}, f32[16,64,128]{2,1,0:T(8,128)S(1)}, u32[]{:S(2)}, u32[]{:S(2)}) collective-permute-start(f32[16,64,128]{2,1,0:T(8,128)S(1)} %all-to-all-done.4.own_ref), channel_id=1, source_target_pairs={{0,1},{1,0},{2,3},{3,2},{4,5},{5,4},{6,7},{7,6},{8,9},{9,8},{10,11... | collective-permute-start | bytes 1572872 | tf_op jit(solution)/shard_map/ppermute | solution.py:23
  115.8 1.5 collective-permute-done.4.other_ref
  117.3 1.7 shard_map.48
  119.0 1.0 copy-done.5
  120.4 0.7 reshape.16
  121.1 3.8 %all-to-all-start.5 = ((f32[8,1,2048]{2,1,0:T(1,128)}), f32[8,1,2048]{2,1,0:T(1,128)S(1)}, u32[]{:S(2)}, u32[]{:S(2)}) async-start(f32[8,1,2048]{2,1,0:T(1,128)} %reshape.16), calls=%async_computation.5 | async-start | bytes 131072 | tf_op jit(solution)/shard_map/all_to_all | solution.py:27
  124.9 5.0 %shard_map.51 = (bf16[1024,896]{1,0:T(8,128)(2,1)S(1)}, bf16[1024,896]{1,0:T(8,128)(2,1)}, bf16[1024,512]{1,0:T(8,128)(2,1)S(1)}, bf16[1024,512]{1,0:T(8,128)(2,1)S(1)}) custom-call(s32[5]{0:T(128)S(1)} %stack.38.at, f32[896,1024]{1,0:T(8,128)} %v_ref.3, f32[1024,512]{1,0:T(8,128)} %u_ref.5), custom_call_target="tpu_custom_call" | custom-call | bytes 12582912 | tf_op jit(solution)/shard_map/pallas_call | solution.py:104
  129.9 1.2 copy-done.4
  131.2 1.0 copy-done.12
  132.2 1.0 copy-done.14
  133.2 1.4 all-to-all-done.5
  134.6 0.5 broadcast
  135.1 0.7 reduce
  135.9 1.1 shard_map.50.rest_4_.cross_ref
  136.9 1.2 copy-done.3
  138.1 9.0 %shard_map.52 = (bf16[8,64,896]{2,1,0:T(8,128)(2,1)}, bf16[2048,896]{1,0:T(8,128)(2,1)}, bf16[2048,896]{1,0:T(8,128)(2,1)}) custom-call(s32[5]{0:T(128)S(1)} %stack.38.at, bf16[128,4096]{1,0:T(8,128)(2,1)} %copy-done.5, bf16[512,896]{1,0:T(8,128)(2,1)} %rest_0_.1, bf16[512,896]{1,0:T(8,128)(2,1)S(1)} %copy-done.3, ...), custom_call_target="tpu_custom_call" | custom-call | flops 939524096 | bytes 12582912 | tf_op jit(solution)/shard_map/pallas_call | solution.py:293
  147.2 9.5 %collective-permute-done.13.rest_3_ = bf16[4,1024,128]{2,1,0:T(8,128)(2,1)} collective-permute-done((bf16[4,1024,128]{2,1,0:T(8,128)(2,1)}, bf16[4,1024,128]{2,1,0:T(8,128)(2,1)}, u32[]{:S(2)}, u32[]{:S(2)}) %collective-permute-start.13) | collective-permute-done | bytes 1048608 | tf_op jit(solution)/shard_map/ppermute | solution.py:23
  156.7 5.2 %shard_map.53 = (f32[32,1024]{1,0:T(8,128)S(1)}, f32[32,1024]{1,0:T(8,128)S(1)}, bf16[1024,2048]{1,0:T(8,128)(2,1)}) custom-call(s32[5]{0:T(128)S(1)} %stack.38.at, f32[32,2048]{1,0:T(8,128)S(1)} %get-tuple-element.32.here_ref, f32[32,2048]{1,0:T(8,128)} %collective-permute-done.5.there_ref, bf16[4,1024,128]{2,1,0:T(8,128)(2,1)} %get-tuple-element.37.rest_0_, ...), custom_call_target="tpu_custom_call" | custom-call | flops 536870912 | bytes 10485760 | tf_op jit(solution)/shard_map/pallas_call | solution.py:229
  161.9 2.2 %collective-permute-start.15 = (f32[32,1024]{1,0:T(8,128)S(1)}, f32[32,1024]{1,0:T(8,128)S(1)}, u32[]{:S(2)}, u32[]{:S(2)}) collective-permute-start(f32[32,1024]{1,0:T(8,128)S(1)} %get-tuple-element.45), channel_id=1, source_target_pairs={{0,1},{1,0},{2,3},{3,2},{4,5},{5,4},{6,7},{7,6},{8,9},{9,8},{10,11... | collective-permute-start | bytes 393224 | tf_op jit(solution)/shard_map/ppermute | solution.py:23
  164.1 1.0 collective-permute-done.15.other_ref
  165.2 0.6 copy-done.6
  166.6 3.3 %collective-permute-start.19 = (bf16[32,1024]{1,0:T(8,128)(2,1)S(1)}, bf16[32,1024]{1,0:T(8,128)(2,1)S(1)}, u32[]{:S(2)}, u32[]{:S(2)}) collective-permute-start(bf16[32,1024]{1,0:T(8,128)(2,1)S(1)} %copy-done.7), channel_id=1, source_target_pairs={{0,4},{2,6},{4,0},{6,2},{1,5},{3,7},{5,1},{7,3},{8,12},{10,14},{12... | collective-permute-start | bytes 196616 | tf_op jit(solution)/shard_map/ppermute | solution.py:23
  170.0 3.3 %collective-permute-start.18 = (bf16[32,1024]{1,0:T(8,128)(2,1)S(1)}, bf16[32,1024]{1,0:T(8,128)(2,1)S(1)}, u32[]{:S(2)}, u32[]{:S(2)}) collective-permute-start(bf16[32,1024]{1,0:T(8,128)(2,1)S(1)} %copy-done.7), channel_id=1, source_target_pairs={{0,6},{2,0},{4,2},{6,4},{1,7},{3,1},{5,3},{7,5},{8,14},{10,8},{12,... | collective-permute-start | bytes 196616 | tf_op jit(solution)/shard_map/ppermute | solution.py:23
  173.3 3.9 %all-to-all-start.6 = ((bf16[8,64,896]{2,1,0:T(8,128)(2,1)}), bf16[8,64,896]{2,1,0:T(8,128)(2,1)S(1)}, u32[]{:S(2)}, u32[]{:S(2)}) async-start(bf16[8,64,896]{2,1,0:T(8,128)(2,1)} %get-tuple-element.49), calls=%async_computation.6 | async-start | bytes 1835008 | tf_op jit(solution)/shard_map/all_to_all | solution.py:369
  177.1 0.9 collective-permute-done.18
  178.0 1.1 collective-permute-done.17
  179.1 0.8 collective-permute-start.20
  179.9 2.0 collective-permute-start.21
  181.9 7.5 %fusion = f32[1024,896]{1,0:T(8,128)S(1)} fusion(bf16[1024,2048]{1,0:T(8,128)(2,1)} %collective-permute-done.16, bf16[2048,896]{1,0:T(8,128)(2,1)} %get-tuple-element.46), kind=kOutput, calls=%fused_computation.2 | convolution fusion | flops 3758096384 | bytes 11534336 | tf_op jit(solution)/shard_map/dot_general | solution.py:31
  189.4 6.3 %convolution_add_fusion.rest_4_.g_ref = f32[1024,896]{1,0:T(8,128)} fusion(f32[1024,896]{1,0:T(8,128)S(1)} %fusion, bf16[1024,2048]{1,0:T(8,128)(2,1)S(1)} %copy-done.16, bf16[2048,896]{1,0:T(8,128)(2,1)S(1)} %copy-done.17), kind=kOutput, calls=%fused_computation | convolution fusion | flops 3759013888 | bytes 15204352 | tf_op jit(solution)/shard_map/dot_general | solution.py:31
  195.8 0.9 shard_map.56.own_ref
  196.7 2.6 %collective-permute-start.23 = (bf16[1024,512]{1,0:T(8,128)(2,1)S(1)}, bf16[1024,512]{1,0:T(8,128)(2,1)S(1)}, u32[]{:S(2)}, u32[]{:S(2)}) collective-permute-start(bf16[1024,512]{1,0:T(8,128)(2,1)S(1)} %shard_map.56.own_ref), channel_id=1, source_target_pairs={{0,1},{1,0},{2,3},{3,2},{4,5},{5,4},{6,7},{7,6},{8,9},{9,8},{10,11... | collective-permute-start | bytes 3145736 | tf_op jit(solution)/shard_map/ppermute | solution.py:23
  199.3 2.3 %collective-permute-done.23.other_ref = bf16[1024,512]{1,0:T(8,128)(2,1)S(1)} collective-permute-done((bf16[1024,512]{1,0:T(8,128)(2,1)S(1)}, bf16[1024,512]{1,0:T(8,128)(2,1)S(1)}, u32[]{:S(2)}, u32[]{:S(2)}) %collective-permute-start.23) | collective-permute-done | bytes 1048608 | tf_op jit(solution)/shard_map/ppermute | solution.py:23
  201.6 1.0 copy-done.19
  202.6 15.6 %shard_map.57 = f32[1024,896]{1,0:T(8,128)} custom-call(f32[1024,896]{1,0:T(8,128)} %convolution_add_fusion.rest_4_.g_ref, bf16[1024,512]{1,0:T(8,128)(2,1)S(1)} %copy-done.13, bf16[1024,512]{1,0:T(8,128)(2,1)S(1)} %copy-done.15, bf16[512,896]{1,0:T(8,128)(2,1)S(1)} %bitcast.19, bf16[1024,512]{1,0:T(8,128)(2,1)S(1)} %shard_map.56.own_ref, ...), custom_call_target="tpu_custom_call" | custom-call | flops 8455716864 | bytes 16777216 | tf_op jit(solution)/shard_map/pallas_call | solution.py:322
  (65 shorter events, 1.8 us)
Async XLA Ops:
  0.1 1.0 copy-start.8
  6.8 11.5 %copy-start.9 = (bf16[128,1024]{1,0:T(8,128)(2,1)S(1)}, bf16[128,1024]{1,0:T(8,128)(2,1)}, u32[]{:S(2)}) copy-start(bf16[128,1024]{1,0:T(8,128)(2,1)} %a_ref.1) | copy-start | bytes 786436
  6.8 6.0 %collective-permute-start = (f32[512,512]{1,0:T(8,128)S(1)}, f32[512,512]{1,0:T(8,128)S(1)}, u32[]{:S(2)}, u32[]{:S(2)}) collective-permute-start(f32[512,512]{1,0:T(8,128)S(1)} %get-tuple-element.29), channel_id=1, source_target_pairs={{0,1},{1,0},{2,3},{3,2},{4,5},{5,4},{6,7},{7,6},{8,9},{9,8},{10,11... | collective-permute-start | bytes 3145736 | tf_op jit(solution)/shard_map/ppermute | solution.py:23
  10.2 24.3 %collective-permute-start.1 = (bf16[512,896]{1,0:T(8,128)(2,1)}, bf16[512,896]{1,0:T(8,128)(2,1)S(1)}, u32[]{:S(2)}, u32[]{:S(2)}) collective-permute-start(bf16[512,896]{1,0:T(8,128)(2,1)} %rest_0_.1), channel_id=1, source_target_pairs={{0,64},{64,128},{128,192},{192,0},{1,65},{65,129},{129,193},{193,1... | collective-permute-start | bytes 2752520 | tf_op jit(solution)/shard_map/ppermute | solution.py:23
  10.2 24.3 %collective-permute-start.2 = (bf16[512,896]{1,0:T(8,128)(2,1)}, bf16[512,896]{1,0:T(8,128)(2,1)S(1)}, u32[]{:S(2)}, u32[]{:S(2)}) collective-permute-start(bf16[512,896]{1,0:T(8,128)(2,1)} %rest_0_.1), channel_id=1, source_target_pairs={{0,192},{64,0},{128,64},{192,128},{1,193},{65,1},{129,65},{193,129... | collective-permute-start | bytes 2752520 | tf_op jit(solution)/shard_map/ppermute | solution.py:23
  12.9 21.6 %collective-permute-start.3 = (bf16[512,896]{1,0:T(8,128)(2,1)}, bf16[512,896]{1,0:T(8,128)(2,1)S(1)}, u32[]{:S(2)}, u32[]{:S(2)}) collective-permute-start(bf16[512,896]{1,0:T(8,128)(2,1)} %rest_0_.1), channel_id=1, source_target_pairs={{0,32},{32,0},{1,33},{33,1},{2,34},{34,2},{3,35},{35,3},{4,36},{36... | collective-permute-start | bytes 2752520 | tf_op jit(solution)/shard_map/ppermute | solution.py:23
  14.0 18.4 %all-to-all-start = ((f32[4,128,512]{2,1,0:T(8,128)}), f32[4,128,512]{2,1,0:T(8,128)}, u32[]{:S(2)}, u32[]{:S(2)}) async-start(f32[4,128,512]{2,1,0:T(8,128)} %bitcast.23), calls=%async_computation | async-start | bytes 2097152 | tf_op jit(solution)/shard_map/all_to_all | solution.py:344
  34.5 64.4 %copy-start.1 = (bf16[512,896]{1,0:T(8,128)(2,1)}, bf16[512,896]{1,0:T(8,128)(2,1)S(1)}, u32[]{:S(2)}) copy-start(bf16[512,896]{1,0:T(8,128)(2,1)S(1)} %collective-permute-done.2.right.rest_3_) | copy-start | bytes 2752516
  34.5 64.4 %copy-start.2 = (bf16[512,896]{1,0:T(8,128)(2,1)}, bf16[512,896]{1,0:T(8,128)(2,1)S(1)}, u32[]{:S(2)}) copy-start(bf16[512,896]{1,0:T(8,128)(2,1)S(1)} %collective-permute-done.3.mate.rest_1_) | copy-start | bytes 2752516
  37.1 9.8 %copy-start.10 = (bf16[1024,128]{1,0:T(8,128)(2,1)}, bf16[1024,128]{1,0:T(8,128)(2,1)S(1)}, u32[]{:S(2)}) copy-start(bf16[1024,128]{1,0:T(8,128)(2,1)S(1)} %get-tuple-element.36.a) | copy-start | bytes 786436
  46.9 14.8 %all-to-all-start.1 = ((f32[4,32,512]{2,1,0:T(8,128)}), f32[4,32,512]{2,1,0:T(8,128)S(1)}, u32[]{:S(2)}, u32[]{:S(2)}) async-start(f32[4,32,512]{2,1,0:T(8,128)} %bitcast.6), calls=%async_computation.1 | async-start | bytes 524288 | tf_op jit(solution)/shard_map/all_to_all | solution.py:354
  53.7 51.2 %collective-permute-start.6 = (bf16[768,896]{1,0:T(8,128)(2,1)}, bf16[768,896]{1,0:T(8,128)(2,1)}, u32[]{:S(2)}, u32[]{:S(2)}) collective-permute-start(bf16[768,896]{1,0:T(8,128)(2,1)} %get-tuple-element.34), channel_id=1, source_target_pairs={{0,64},{64,128},{128,192},{192,0},{1,65},{65,129},{129,193},{193,1... | collective-permute-start | bytes 4128776 | tf_op jit(solution)/shard_map/ppermute | solution.py:23
  53.7 51.2 %collective-permute-start.7 = (bf16[768,896]{1,0:T(8,128)(2,1)}, bf16[768,896]{1,0:T(8,128)(2,1)}, u32[]{:S(2)}, u32[]{:S(2)}) collective-permute-start(bf16[768,896]{1,0:T(8,128)(2,1)} %get-tuple-element.35), channel_id=1, source_target_pairs={{0,192},{64,0},{128,64},{192,128},{1,193},{65,1},{129,65},{193,129... | collective-permute-start | bytes 4128776 | tf_op jit(solution)/shard_map/ppermute | solution.py:23
  61.7 0.9 copy-start.18
  62.6 35.4 %all-to-all-start.4 = ((f32[16,64,128]{2,1,0:T(8,128)}), f32[16,64,128]{2,1,0:T(8,128)S(1)}, u32[]{:S(2)}, u32[]{:S(2)}) async-start(f32[16,64,128]{2,1,0:T(8,128)} %broadcast_in_dim.10), calls=%async_computation.4 | async-start | bytes 1048576 | tf_op jit(solution)/shard_map/all_to_all | solution.py:27
  67.4 37.4 %collective-permute-start.8 = (bf16[1024,128]{1,0:T(8,128)(2,1)}, bf16[1024,128]{1,0:T(8,128)(2,1)}, u32[]{:S(2)}, u32[]{:S(2)}) collective-permute-start(bf16[1024,128]{1,0:T(8,128)(2,1)} %copy-done.10), channel_id=1, source_target_pairs={{0,2},{2,4},{4,6},{6,0},{1,3},{3,5},{5,7},{7,1},{8,10},{10,12},{12... | collective-permute-start | bytes 786440 | tf_op jit(solution)/shard_map/ppermute | solution.py:23
  69.6 35.2 %collective-permute-start.9 = (bf16[1024,128]{1,0:T(8,128)(2,1)}, bf16[1024,128]{1,0:T(8,128)(2,1)}, u32[]{:S(2)}, u32[]{:S(2)}) collective-permute-start(bf16[1024,128]{1,0:T(8,128)(2,1)} %copy-done.10), channel_id=1, source_target_pairs={{0,6},{2,0},{4,2},{6,4},{1,7},{3,1},{5,3},{7,5},{8,14},{10,8},{12,... | collective-permute-start | bytes 786440 | tf_op jit(solution)/shard_map/ppermute | solution.py:23
  71.0 33.8 %collective-permute-start.10 = (bf16[1024,128]{1,0:T(8,128)(2,1)}, bf16[1024,128]{1,0:T(8,128)(2,1)}, u32[]{:S(2)}, u32[]{:S(2)}) collective-permute-start(bf16[1024,128]{1,0:T(8,128)(2,1)} %copy-done.10), channel_id=1, source_target_pairs={{0,4},{2,6},{4,0},{6,2},{1,5},{3,7},{5,1},{7,3},{8,12},{10,14},{12... | collective-permute-start | bytes 786440 | tf_op jit(solution)/shard_map/ppermute | solution.py:23
  98.8 16.9 %all-to-all-start.2 = ((f32[8,32,512]{2,1,0:T(8,128)}), f32[8,32,512]{2,1,0:T(8,128)S(1)}, u32[]{:S(2)}, u32[]{:S(2)}) async-start(f32[8,32,512]{2,1,0:T(8,128)} %broadcast_in_dim.9), calls=%async_computation.2 | async-start | bytes 1048576 | tf_op jit(solution)/shard_map/all_to_all | solution.py:27
  104.9 1.0 copy-start.11
  108.6 38.6 %collective-permute-start.11 = (bf16[4,1024,128]{2,1,0:T(8,128)(2,1)}, bf16[4,1024,128]{2,1,0:T(8,128)(2,1)}, u32[]{:S(2)}, u32[]{:S(2)}) collective-permute-start(bf16[4,1024,128]{2,1,0:T(8,128)(2,1)} %get-tuple-element.37.rest_0_), channel_id=1, source_target_pairs={{0,8},{8,16},{16,24},{24,0},{1,9},{9,17},{17,25},{25,1},{2,10},{10... | collective-permute-start | bytes 3145736 | tf_op jit(solution)/shard_map/ppermute | solution.py:23
  109.5 37.6 %collective-permute-start.12 = (bf16[4,1024,128]{2,1,0:T(8,128)(2,1)}, bf16[4,1024,128]{2,1,0:T(8,128)(2,1)}, u32[]{:S(2)}, u32[]{:S(2)}) collective-permute-start(bf16[4,1024,128]{2,1,0:T(8,128)(2,1)} %get-tuple-element.37.rest_0_), channel_id=1, source_target_pairs={{0,24},{8,0},{16,8},{24,16},{1,25},{9,1},{17,9},{25,17},{2,26},{10... | collective-permute-start | bytes 3145736 | tf_op jit(solution)/shard_map/ppermute | solution.py:23
  111.3 45.4 %collective-permute-start.13 = (bf16[4,1024,128]{2,1,0:T(8,128)(2,1)}, bf16[4,1024,128]{2,1,0:T(8,128)(2,1)}, u32[]{:S(2)}, u32[]{:S(2)}) collective-permute-start(bf16[4,1024,128]{2,1,0:T(8,128)(2,1)} %get-tuple-element.37.rest_0_), channel_id=1, source_target_pairs={{0,16},{8,24},{16,0},{24,8},{1,17},{9,25},{17,1},{25,9},{2,18},{10... | collective-permute-start | bytes 3145736 | tf_op jit(solution)/shard_map/ppermute | solution.py:23
  112.5 24.4 %collective-permute-start.14 = (bf16[512,896]{1,0:T(8,128)(2,1)}, bf16[512,896]{1,0:T(8,128)(2,1)}, u32[]{:S(2)}, u32[]{:S(2)}) collective-permute-start(bf16[512,896]{1,0:T(8,128)(2,1)} %get-tuple-element.41), channel_id=1, source_target_pairs={{0,32},{32,0},{1,33},{33,1},{2,34},{34,2},{3,35},{35,3},{4,36},{36... | collective-permute-start | bytes 2752520 | tf_op jit(solution)/shard_map/ppermute | solution.py:23
  113.3 4.0 %collective-permute-start.4 = (f32[16,64,128]{2,1,0:T(8,128)S(1)}, f32[16,64,128]{2,1,0:T(8,128)S(1)}, u32[]{:S(2)}, u32[]{:S(2)}) collective-permute-start(f32[16,64,128]{2,1,0:T(8,128)S(1)} %all-to-all-done.4.own_ref), channel_id=1, source_target_pairs={{0,1},{1,0},{2,3},{3,2},{4,5},{5,4},{6,7},{7,6},{8,9},{9,8},{10,11... | collective-permute-start | bytes 1572872 | tf_op jit(solution)/shard_map/ppermute | solution.py:23
  119.0 1.0 copy-start.5
  120.0 15.9 %copy-start = (f32[1024,512]{1,0:T(8,128)S(1)}, f32[1024,512]{1,0:T(8,128)}, u32[]{:S(2)}) copy-start(f32[1024,512]{1,0:T(8,128)} %u_ref.5) | copy-start | bytes 6291460
  120.0 27.2 %collective-permute-start.5 = (f32[32,2048]{1,0:T(8,128)}, f32[32,2048]{1,0:T(8,128)}, u32[]{:S(2)}, u32[]{:S(2)}) collective-permute-start(f32[32,2048]{1,0:T(8,128)} %get-tuple-element.33), channel_id=1, source_target_pairs={{0,1},{1,0},{2,3},{3,2},{4,5},{5,4},{6,7},{7,6},{8,9},{9,8},{10,11... | collective-permute-start | bytes 786440 | tf_op jit(solution)/shard_map/ppermute | solution.py:23
  121.1 13.5 %all-to-all-start.5 = ((f32[8,1,2048]{2,1,0:T(1,128)}), f32[8,1,2048]{2,1,0:T(1,128)S(1)}, u32[]{:S(2)}, u32[]{:S(2)}) async-start(f32[8,1,2048]{2,1,0:T(1,128)} %reshape.16), calls=%async_computation.5 | async-start | bytes 131072 | tf_op jit(solution)/shard_map/all_to_all | solution.py:27
  129.9 1.2 copy-start.4
  131.2 1.0 copy-start.12
  132.2 1.0 copy-start.14
  136.9 1.2 copy-start.3
  161.9 3.2 %collective-permute-start.15 = (f32[32,1024]{1,0:T(8,128)S(1)}, f32[32,1024]{1,0:T(8,128)S(1)}, u32[]{:S(2)}, u32[]{:S(2)}) collective-permute-start(f32[32,1024]{1,0:T(8,128)S(1)} %get-tuple-element.45), channel_id=1, source_target_pairs={{0,1},{1,0},{2,3},{3,2},{4,5},{5,4},{6,7},{7,6},{8,9},{9,8},{10,11... | collective-permute-start | bytes 393224 | tf_op jit(solution)/shard_map/ppermute | solution.py:23
  165.2 0.6 copy-start.6
  165.8 0.8 copy-start.7
  165.8 16.1 %collective-permute-start.16 = (bf16[1024,2048]{1,0:T(8,128)(2,1)}, bf16[1024,2048]{1,0:T(8,128)(2,1)}, u32[]{:S(2)}, u32[]{:S(2)}) collective-permute-start(bf16[1024,2048]{1,0:T(8,128)(2,1)} %shard_map.55), channel_id=1, source_target_pairs={{0,1},{1,0},{2,3},{3,2},{4,5},{5,4},{6,7},{7,6},{8,9},{9,8},{10,11... | collective-permute-start | bytes 12582920 | tf_op jit(solution)/shard_map/ppermute | solution.py:23
  166.6 10.5 %collective-permute-start.19 = (bf16[32,1024]{1,0:T(8,128)(2,1)S(1)}, bf16[32,1024]{1,0:T(8,128)(2,1)S(1)}, u32[]{:S(2)}, u32[]{:S(2)}) collective-permute-start(bf16[32,1024]{1,0:T(8,128)(2,1)S(1)} %copy-done.7), channel_id=1, source_target_pairs={{0,4},{2,6},{4,0},{6,2},{1,5},{3,7},{5,1},{7,3},{8,12},{10,14},{12... | collective-permute-start | bytes 196616 | tf_op jit(solution)/shard_map/ppermute | solution.py:23
  170.0 8.0 %collective-permute-start.18 = (bf16[32,1024]{1,0:T(8,128)(2,1)S(1)}, bf16[32,1024]{1,0:T(8,128)(2,1)S(1)}, u32[]{:S(2)}, u32[]{:S(2)}) collective-permute-start(bf16[32,1024]{1,0:T(8,128)(2,1)S(1)} %copy-done.7), channel_id=1, source_target_pairs={{0,6},{2,0},{4,2},{6,4},{1,7},{3,1},{5,3},{7,5},{8,14},{10,8},{12,... | collective-permute-start | bytes 196616 | tf_op jit(solution)/shard_map/ppermute | solution.py:23
  173.3 5.8 %collective-permute-start.17 = (bf16[32,1024]{1,0:T(8,128)(2,1)S(1)}, bf16[32,1024]{1,0:T(8,128)(2,1)S(1)}, u32[]{:S(2)}, u32[]{:S(2)}) collective-permute-start(bf16[32,1024]{1,0:T(8,128)(2,1)S(1)} %copy-done.7), channel_id=1, source_target_pairs={{0,2},{2,4},{4,6},{6,0},{1,3},{3,5},{5,7},{7,1},{8,10},{10,12},{12... | collective-permute-start | bytes 196616 | tf_op jit(solution)/shard_map/ppermute | solution.py:23
  173.3 22.5 %all-to-all-start.6 = ((bf16[8,64,896]{2,1,0:T(8,128)(2,1)}), bf16[8,64,896]{2,1,0:T(8,128)(2,1)S(1)}, u32[]{:S(2)}, u32[]{:S(2)}) async-start(bf16[8,64,896]{2,1,0:T(8,128)(2,1)} %get-tuple-element.49), calls=%async_computation.6 | async-start | bytes 1835008 | tf_op jit(solution)/shard_map/all_to_all | solution.py:369
  179.1 16.6 %collective-permute-start.20 = (bf16[4,32,1024]{2,1,0:T(8,128)(2,1)S(1)}, bf16[4,32,1024]{2,1,0:T(8,128)(2,1)S(1)}, u32[]{:S(2)}, u32[]{:S(2)}) collective-permute-start(bf16[4,32,1024]{2,1,0:T(8,128)(2,1)S(1)} %pad_maximum_fusion.rest_0_), channel_id=1, source_target_pairs={{0,8},{8,16},{16,24},{24,0},{1,9},{9,17},{17,25},{25,1},{2,10},{10... | collective-permute-start | bytes 786440 | tf_op jit(solution)/shard_map/ppermute | solution.py:23
  179.9 15.9 %collective-permute-start.21 = (bf16[4,32,1024]{2,1,0:T(8,128)(2,1)S(1)}, bf16[4,32,1024]{2,1,0:T(8,128)(2,1)S(1)}, u32[]{:S(2)}, u32[]{:S(2)}) collective-permute-start(bf16[4,32,1024]{2,1,0:T(8,128)(2,1)S(1)} %pad_maximum_fusion.rest_0_), channel_id=1, source_target_pairs={{0,24},{8,0},{16,8},{24,16},{1,25},{9,1},{17,9},{25,17},{2,26},{10... | collective-permute-start | bytes 786440 | tf_op jit(solution)/shard_map/ppermute | solution.py:23
  181.9 13.9 %collective-permute-start.22 = (bf16[4,32,1024]{2,1,0:T(8,128)(2,1)S(1)}, bf16[4,32,1024]{2,1,0:T(8,128)(2,1)S(1)}, u32[]{:S(2)}, u32[]{:S(2)}) collective-permute-start(bf16[4,32,1024]{2,1,0:T(8,128)(2,1)S(1)} %pad_maximum_fusion.rest_0_), channel_id=1, source_target_pairs={{0,16},{8,24},{16,0},{24,8},{1,17},{9,25},{17,1},{25,9},{2,18},{10... | collective-permute-start | bytes 786440 | tf_op jit(solution)/shard_map/ppermute | solution.py:23
  181.9 7.5 %copy-start.16 = (bf16[1024,2048]{1,0:T(8,128)(2,1)S(1)}, bf16[1024,2048]{1,0:T(8,128)(2,1)}, u32[]{:S(2)}) copy-start(bf16[1024,2048]{1,0:T(8,128)(2,1)} %shard_map.55) | copy-start | bytes 12582916
  181.9 7.5 %copy-start.17 = (bf16[2048,896]{1,0:T(8,128)(2,1)S(1)}, bf16[2048,896]{1,0:T(8,128)(2,1)}, u32[]{:S(2)}) copy-start(bf16[2048,896]{1,0:T(8,128)(2,1)} %get-tuple-element.42.rest_6_) | copy-start | bytes 11010052
  195.7 6.8 %copy-start.13 = (bf16[1024,512]{1,0:T(8,128)(2,1)S(1)}, bf16[1024,512]{1,0:T(8,128)(2,1)}, u32[]{:S(2)}) copy-start(bf16[1024,512]{1,0:T(8,128)(2,1)} %copy-done.12) | copy-start | bytes 3145732
  195.8 6.8 %copy-start.15 = (bf16[1024,512]{1,0:T(8,128)(2,1)S(1)}, bf16[1024,512]{1,0:T(8,128)(2,1)}, u32[]{:S(2)}) copy-start(bf16[1024,512]{1,0:T(8,128)(2,1)} %copy-done.14) | copy-start | bytes 3145732
  196.7 4.8 %collective-permute-start.23 = (bf16[1024,512]{1,0:T(8,128)(2,1)S(1)}, bf16[1024,512]{1,0:T(8,128)(2,1)S(1)}, u32[]{:S(2)}, u32[]{:S(2)}) collective-permute-start(bf16[1024,512]{1,0:T(8,128)(2,1)S(1)} %shard_map.56.own_ref), channel_id=1, source_target_pairs={{0,1},{1,0},{2,3},{3,2},{4,5},{5,4},{6,7},{7,6},{8,9},{9,8},{10,11... | collective-permute-start | bytes 3145736 | tf_op jit(solution)/shard_map/ppermute | solution.py:23
  201.6 1.0 copy-start.19
